TPU v7x, 32 devices: a whole 2x2x4 slice. The times are simulated.
32 devices in a mesh: gx: 16 (over z, y, core), gy: 2 (over x).
Axes of the slice: x: 2, y: 2, z: 4, core: 2. Of those that a mesh axis runs over, the one named last changes fastest.
Arguments:
- gas_state: float32 [5, 128, 16, 256], P(None, 'gx', 'gy'), may hold values from -3 to 3
- pressure_guess: float32 [128, 16, 256], P('gx', 'gy'), may hold values from -6 to 6
- drop_motion: float32 [4, 16, 8192], P(None, 'gx', 'gy'), may hold values from -6 to 6
- drop_size: float32 [16, 8192], P('gx', 'gy'), may hold values from 0.5 to 2
- drop_cell: int32 [16, 8192], P('gx', 'gy'), may hold values from 0 to 16383
- drop_target: int32 [16, 8192], P('gx', 'gy'), may hold values from -1 to 4, as said below
- spray_on: int32 [16, 16], P('gx', 'gy'), may hold values 0 or 1
- spray_time: int32 [16, 16], P('gx', 'gy'), may hold values from 0 to 100
- spray_cell: int32 [16, 16], P('gx', 'gy'), may hold values from 0 to 16383
Outputs:
- gas_next: float32 [5, 128, 16, 256], P(None, 'gx', 'gy')
- pressure: float32 [128, 16, 256], P('gx', 'gy')
- drop_kept: float32 [5, 16, 8192], P(None, 'gx', 'gy')
- drop_arrived: float32 [4, 5, 16, 1024], P(None, None, 'gx', 'gy')
Inputs may be any that keep to these rules, and one draw needn't show every extreme that they name: `drop_target`: in each device's 4096 slots at most 512 droplets have any one of the targets 0, 1, 2, 3, and on every device one of these targets has exactly 512.
All inputs are finite; a program needn't handle non-finite values. No bound on the sum of `spray_on` on one device may be relied on, other than what follows from the above.
Results may differ from a plain program's by a relative error of at most 0.00002.
Values sent between devices are 32-bit elements; how exact they have to be, the bound alone decides.
A program may use at most 128 MiB of HBM per device.

v0:
```python
import jax
import jax.numpy as jnp
from jax import lax
from jax.sharding import PartitionSpec as P

ITERS = 8
CAP = 512


TIME_STEP = 0.2
DIFFUSION = 0.1
DRAG_TIME = 0.5
HEAT_TIME = 1.0
GRAVITY = 1.0
VAPOUR_RATE = 0.5
DRAG_COUPLING = 0.5
LATENT = 2.0
VAPOUR_YIELD = 1.0
SPRAY_RATE = 3.0
CLOCK = 100.0
SPRAY_RAMP = 50.0


def padded_2(shard, sides, width):
    for axis, dim in sides:
        peers, length = (lax.axis_size(axis), shard.shape[dim])
        up = [(i, (i + 1) % peers) for i in range(peers - 1)]
        down = [(j, i) for i, j in up]
        last = lax.slice_in_dim(shard, length - width, length, axis=dim)
        leading = lax.slice_in_dim(shard, 0, width, axis=dim)
        before = lax.ppermute(last, axis, up)
        after = lax.ppermute(leading, axis, down)
        shard = jnp.concatenate([before, shard, after], axis=dim)
    return shard


def shifted(shard, axis, by):
    peers = lax.axis_size(axis)
    pairs = [(i, i + by) for i in range(peers) if 0 <= i + by < peers]
    return lax.ppermute(shard, axis, pairs)


def window(padded, along_x, along_y, along_z):
    a = padded.shape[-3] - 4
    b = padded.shape[-2] - 4
    c = padded.shape[-1] - 4
    return padded[
        ...,
        2 + along_x : 2 + along_x + a,
        2 + along_y : 2 + along_y + b,
        2 + along_z : 2 + along_z + c,
    ]


def gradient(padded, along_x, along_y, along_z):
    near = window(padded, along_x, along_y, along_z) - window(padded, -along_x, -along_y, -along_z)
    far = window(padded, 2 * along_x, 2 * along_y, 2 * along_z) - window(
        padded, -2 * along_x, -2 * along_y, -2 * along_z
    )
    return (8.0 * near - far) / 12.0


def predict(padded):
    speed_x = window(padded[0], 0, 0, 0)
    speed_y = window(padded[1], 0, 0, 0)
    speed_z = window(padded[2], 0, 0, 0)
    results = []
    for field in range(padded.shape[0]):
        single = padded[field]
        centre = window(single, 0, 0, 0)
        laplace = window(single, 1, 0, 0) + window(single, -1, 0, 0) + window(single, 0, 1, 0)
        laplace = (
            laplace
            + window(single, 0, -1, 0)
            + window(single, 0, 0, 1)
            + window(single, 0, 0, -1)
            - 6.0 * centre
        )
        transport = (
            speed_x * gradient(single, 1, 0, 0)
            + speed_y * gradient(single, 0, 1, 0)
            + speed_z * gradient(single, 0, 0, 1)
        )
        results.append(centre + TIME_STEP * (DIFFUSION * laplace - transport))
    return jnp.stack(results)


def divergence(flow_x, flow_y, vertical):
    lifted = jnp.pad(vertical, ((0, 0), (0, 0), (1, 1)))
    spread = 0.5 * (flow_x[2:, 1:-1] - flow_x[:-2, 1:-1]) + 0.5 * (
        flow_y[1:-1, 2:] - flow_y[1:-1, :-2]
    )
    spread = spread + 0.5 * (lifted[:, :, 2:] - lifted[:, :, :-2])
    return spread / TIME_STEP


def sweep(bordered, source):
    inner = bordered[1:-1, 1:-1]
    lifted = jnp.pad(inner, ((0, 0), (0, 0), (1, 1)))
    beside_all = bordered[2:, 1:-1] + bordered[:-2, 1:-1] + bordered[1:-1, 2:] + bordered[1:-1, :-2]
    beside_all = beside_all + lifted[:, :, 2:] + lifted[:, :, :-2]
    return (beside_all - source) / 6.0


def correct(star, bordered):
    inner = bordered[1:-1, 1:-1]
    lifted = jnp.pad(inner, ((0, 0), (0, 0), (1, 1)))
    flow_x = star[0] - TIME_STEP * 0.5 * (bordered[2:, 1:-1] - bordered[:-2, 1:-1])
    flow_y = star[1] - TIME_STEP * 0.5 * (bordered[1:-1, 2:] - bordered[1:-1, :-2])
    vertical = star[2] - TIME_STEP * 0.5 * (lifted[:, :, 2:] - lifted[:, :, :-2])
    return jnp.concatenate([jnp.stack([flow_x, flow_y, vertical]), star[3:]], axis=0)


def droplets(motion, diameter, local):
    excess = local[3] - motion[3]
    vapour = VAPOUR_RATE * diameter * jax.nn.sigmoid(excess)
    renewed = jnp.stack(
        [
            motion[0] + TIME_STEP * (local[0] - motion[0]) / DRAG_TIME,
            motion[1] + TIME_STEP * (local[1] - motion[1]) / DRAG_TIME,
            motion[2] + TIME_STEP * ((local[2] - motion[2]) / DRAG_TIME - GRAVITY),
            motion[3] + TIME_STEP * excess / HEAT_TIME,
            diameter - TIME_STEP * vapour,
        ]
    )
    sources = jnp.stack(
        [
            DRAG_COUPLING * diameter * diameter * (motion[2] - local[2]),
            -LATENT * vapour,
            VAPOUR_YIELD * vapour,
        ]
    )
    return (renewed, sources)


def spray(flags, times):
    ramp = jnp.clip((CLOCK - times.astype(jnp.float32)) / SPRAY_RAMP, 0.0, 1.0)
    strength = SPRAY_RATE * ramp * flags.astype(jnp.float32)
    return jnp.stack([-strength, -strength, jnp.zeros_like(strength)])


def add_sources(star, sources):
    return jnp.concatenate([star[:2], star[2:] + TIME_STEP * sources], axis=0)


def body(
    gas_state,
    pressure_guess,
    drop_motion,
    drop_size,
    drop_cell,
    drop_target,
    spray_on,
    spray_time,
    spray_cell,
):
    fields, wide_x, wide_y, depth = gas_state.shape
    volume = wide_x * wide_y * depth
    flat = gas_state.reshape(fields, volume)
    cells = drop_cell[0]
    target = drop_target[0]
    local = flat[:, cells]
    renewed, drop_sources = droplets(drop_motion[:, 0], drop_size[0], local)
    drop_sources = jnp.where((target >= 0)[None], drop_sources, 0.0)
    sources = jnp.zeros((3, volume), jnp.float32).at[:, cells].add(drop_sources)
    sources = sources.at[:, spray_cell[0]].add(spray(spray_on[0], spray_time[0]))
    sources = sources.reshape(3, wide_x, wide_y, depth)
    padded = padded_2(gas_state, (("gx", 1), ("gy", 2)), 2)
    padded = jnp.pad(padded, ((0, 0), (0, 0), (0, 0), (2, 2)))
    star = add_sources(predict(padded), sources)
    flows = padded_2(star[:2], (("gx", 1), ("gy", 2)), 1)
    source = divergence(flows[0], flows[1], star[2])
    field = pressure_guess
    for turn in range(ITERS):
        bordered = padded_2(field, (("gx", 0), ("gy", 1)), 1)
        field = sweep(bordered, source)
    final_rim = padded_2(field, (("gx", 0), ("gy", 1)), 1)
    gas_next = correct(star, final_rim)
    parcels = []
    for heading in range(4):
        chosen = target == heading
        order = jnp.cumsum(chosen.astype(jnp.int32)) - 1
        place = jnp.where(chosen, order, CAP)
        parcel = jnp.zeros((5, CAP + 1), jnp.float32).at[:, place].set(renewed)
        parcels.append(parcel[:, None, :CAP])
    arrived = jnp.stack(
        [
            shifted(parcels[0], "gx", 1),
            shifted(parcels[1], "gx", -1),
            shifted(parcels[2], "gy", 1),
            shifted(parcels[3], "gy", -1),
        ]
    )
    drop_kept = jnp.where((target == 4)[None], renewed, 0.0)[:, None, :]
    return (gas_next, field, drop_kept, arrived)


def solution(mesh):
    in_specs = (
        P(None, "gx", "gy", None),
        P("gx", "gy", None),
        P(None, "gx", "gy"),
        P("gx", "gy"),
        P("gx", "gy"),
        P("gx", "gy"),
        P("gx", "gy"),
        P("gx", "gy"),
        P("gx", "gy"),
    )
    out_specs = (
        P(None, "gx", "gy", None),
        P("gx", "gy", None),
        P(None, "gx", "gy"),
        P(None, None, "gx", "gy"),
    )
    return jax.shard_map(body, mesh=mesh, in_specs=in_specs, out_specs=out_specs, check_vma=False)
```

profile of v0, /device:TPU:1, one launch (start us, length us, event | category | flops | bytes accessed | tf_op | source)
XLA Modules:
  0.0 280.2 jit_solution(16691652317755811817)
XLA Ops:
  1.6 4.5 %collective-permute-start = (f32[5,2,8,256]{3,2,1,0:T(8,128)S(1)}, f32[5,2,8,256]{3,2,1,0:T(8,128)S(1)}, u32[]{:S(2)}, u32[]{:S(2)}) collective-permute-start(f32[5,2,8,256]{3,2,1,0:T(8,128)S(1)} %get-tuple-element.45), channel_id=1, source_target_pairs={{0,2},{2,4},{4,6},{6,8},{8,10},{10,12},{12,14},{14,16},{16,18},{18... | collective-permute-start | bytes 245768 | tf_op jit(solution)/shard_map/ppermute | solution.py:31
  6.1 1.9 collective-permute-start.1
  8.8 3.6 %collective-permute-start.5 = (f32[1,8,256]{2,1,0:T(8,128)S(1)}, f32[1,8,256]{2,1,0:T(8,128)S(1)}, u32[]{:S(2)}, u32[]{:S(2)}) collective-permute-start(f32[1,8,256]{2,1,0:T(8,128)S(1)} %get-tuple-element.88), channel_id=1, source_target_pairs={{0,2},{2,4},{4,6},{6,8},{8,10},{10,12},{12,14},{14,16},{16,18},{18... | collective-permute-start | bytes 24584 | tf_op jit(solution)/shard_map/ppermute | solution.py:31
  12.4 1.9 collective-permute-start.4
  14.4 5.9 %copy.86 = f32[5,8,8,256]{0,3,2,1:T(8,128)} copy(f32[5,8,8,256]{3,2,1,0:T(8,128)} %param.9) | data formatting | bytes 655360 | tf_op args[0]
  20.4 14.2 %gather_fusion = f32[4096,5]{1,0:T(8,128)S(1)} fusion(f32[5,16384]{0,1:T(8,128)} %bitcast.126, s32[4096]{0:T(1024)S(1)} %broadcast_clamp_fusion), kind=kCustom, calls=%fused_computation | custom fusion | bytes 180224 | tf_op jit(solution)/shard_map/gather | solution.py:162
  36.4 26.1 %scatter_custom_fusion = f32[3,16384]{0,1:T(8,128)} fusion(s32[4096]{0:T(1024)S(1)} %bitcast.147, f32[4096,3]{1,0:T(8,128)S(1)} %copy.88, f32[]{:T(128)} %constant.73.clone.1), kind=kCustom, calls=%fused_computation.8 | custom fusion | flops 12288 | bytes 196612 | tf_op jit(solution)/shard_map/scatter-add | solution.py:165
  62.7 7.2 %scatter_fusion = f32[3,16384]{0,1:T(8,128)} fusion(f32[3,16384]{0,1:T(8,128)} %scatter_custom_fusion, s32[8]{0:T(128)S(1)} %fusion.164, f32[8,3]{1,0:T(8,128)S(1)} %copy.89), kind=kCustom, calls=%fused_computation.2 | custom fusion | flops 24 | bytes 320 | tf_op jit(solution)/shard_map/scatter-add | solution.py:166
  69.9 5.8 %broadcast_multiply_fusion = f32[3,16384]{0,1:T(8,128)} fusion(f32[3,16384]{0,1:T(8,128)} %scatter_fusion), kind=kLoop, calls=%fused_computation.7 | loop fusion | flops 49152 | bytes 393216 | tf_op jit(solution)/shard_map/mul | solution.py:143
  75.7 5.3 %copy.90 = f32[3,8,8,256]{3,2,1,0:T(8,128)S(1)} copy(f32[3,8,8,256]{0,3,2,1:T(8,128)} %bitcast.125) | data formatting | bytes 393216 | tf_op jit(solution)/shard_map/mul | solution.py:143
  81.2 1.3 collective-permute-start.3
  82.5 4.0 %collective-permute-start.2 = (f32[5,12,2,256]{3,2,1,0:T(2,128)S(1)}, f32[5,12,2,256]{3,2,1,0:T(2,128)S(1)}, u32[]{:S(2)}, u32[]{:S(2)}) collective-permute-start(f32[5,12,2,256]{3,2,1,0:T(2,128)S(1)} %get-tuple-element.40), channel_id=1, source_target_pairs={{0,1},{2,3},{4,5},{6,7},{8,9},{10,11},{12,13},{14,15},{16,17},{18,... | collective-permute-start | bytes 368648 | tf_op jit(solution)/shard_map/ppermute | solution.py:31
  86.6 1.3 collective-permute-start.7
  87.9 1.3 collective-permute-start.6
  91.9 1.9 collective-permute-start.9
  93.8 4.9 %collective-permute-start.8 = (f32[2,1,8,256]{3,2,1,0:T(8,128)S(1)}, f32[2,1,8,256]{3,2,1,0:T(8,128)S(1)}, u32[]{:S(2)}, u32[]{:S(2)}) collective-permute-start(f32[2,1,8,256]{3,2,1,0:T(8,128)S(1)} %get-tuple-element.48), channel_id=1, source_target_pairs={{0,2},{2,4},{4,6},{6,8},{8,10},{10,12},{12,14},{14,16},{16,18},{18... | collective-permute-start | bytes 49160 | tf_op jit(solution)/shard_map/ppermute | solution.py:31
  99.6 1.3 collective-permute-start.11
  100.9 4.1 %collective-permute-start.10 = (f32[2,10,1,256]{3,2,1,0:T(1,128)S(1)}, f32[2,10,1,256]{3,2,1,0:T(1,128)S(1)}, u32[]{:S(2)}, u32[]{:S(2)}) collective-permute-start(f32[2,10,1,256]{3,2,1,0:T(1,128)S(1)} %get-tuple-element.46), channel_id=1, source_target_pairs={{0,1},{2,3},{4,5},{6,7},{8,9},{10,11},{12,13},{14,15},{16,17},{18,... | collective-permute-start | bytes 61448 | tf_op jit(solution)/shard_map/ppermute | solution.py:31
  106.2 1.9 collective-permute-start.12
  108.1 5.2 %collective-permute-start.13 = (f32[1,8,256]{2,1,0:T(8,128)S(1)}, f32[1,8,256]{2,1,0:T(8,128)S(1)}, u32[]{:S(2)}, u32[]{:S(2)}) collective-permute-start(f32[1,8,256]{2,1,0:T(8,128)S(1)} %get-tuple-element.85), channel_id=1, source_target_pairs={{0,2},{2,4},{4,6},{6,8},{8,10},{10,12},{12,14},{14,16},{16,18},{18... | collective-permute-start | bytes 24584 | tf_op jit(solution)/shard_map/ppermute | solution.py:31
  114.1 3.9 %collective-permute-start.15 = (f32[10,1,256]{2,1,0:T(1,128)S(1)}, f32[10,1,256]{2,1,0:T(1,128)S(1)}, u32[]{:S(2)}, u32[]{:S(2)}) collective-permute-start(f32[10,1,256]{2,1,0:T(1,128)S(1)} %get-tuple-element.67), channel_id=1, source_target_pairs={{0,1},{2,3},{4,5},{6,7},{8,9},{10,11},{12,13},{14,15},{16,17},{18,... | collective-permute-start | bytes 30728 | tf_op jit(solution)/shard_map/ppermute | solution.py:31
  118.1 1.3 collective-permute-start.14
  119.5 3.0 %collective-permute-done.14 = f32[10,1,256]{2,1,0:T(1,128)S(1)} collective-permute-done((f32[10,1,256]{2,1,0:T(1,128)S(1)}, f32[10,1,256]{2,1,0:T(1,128)S(1)}, u32[]{:S(2)}, u32[]{:S(2)}) %collective-permute-start.14) | collective-permute-done | bytes 10272 | tf_op jit(solution)/shard_map/ppermute | solution.py:32
  122.6 1.9 collective-permute-start.16
  124.5 5.6 %collective-permute-start.17 = (f32[1,8,256]{2,1,0:T(8,128)S(1)}, f32[1,8,256]{2,1,0:T(8,128)S(1)}, u32[]{:S(2)}, u32[]{:S(2)}) collective-permute-start(f32[1,8,256]{2,1,0:T(8,128)S(1)} %get-tuple-element.83), channel_id=1, source_target_pairs={{0,2},{2,4},{4,6},{6,8},{8,10},{10,12},{12,14},{14,16},{16,18},{18... | collective-permute-start | bytes 24584 | tf_op jit(solution)/shard_map/ppermute | solution.py:31
  131.0 1.3 collective-permute-start.19
  132.3 1.3 collective-permute-start.18
  133.7 3.0 %collective-permute-done.18 = f32[10,1,256]{2,1,0:T(1,128)S(1)} collective-permute-done((f32[10,1,256]{2,1,0:T(1,128)S(1)}, f32[10,1,256]{2,1,0:T(1,128)S(1)}, u32[]{:S(2)}, u32[]{:S(2)}) %collective-permute-start.18) | collective-permute-done | bytes 10272 | tf_op jit(solution)/shard_map/ppermute | solution.py:32
  136.8 1.9 collective-permute-start.20
  138.8 5.6 %collective-permute-start.21 = (f32[1,8,256]{2,1,0:T(8,128)S(1)}, f32[1,8,256]{2,1,0:T(8,128)S(1)}, u32[]{:S(2)}, u32[]{:S(2)}) collective-permute-start(f32[1,8,256]{2,1,0:T(8,128)S(1)} %get-tuple-element.81), channel_id=1, source_target_pairs={{0,2},{2,4},{4,6},{6,8},{8,10},{10,12},{12,14},{14,16},{16,18},{18... | collective-permute-start | bytes 24584 | tf_op jit(solution)/shard_map/ppermute | solution.py:31
  145.2 1.4 collective-permute-start.23
  146.6 1.3 collective-permute-start.22
  148.0 3.0 %collective-permute-done.22 = f32[10,1,256]{2,1,0:T(1,128)S(1)} collective-permute-done((f32[10,1,256]{2,1,0:T(1,128)S(1)}, f32[10,1,256]{2,1,0:T(1,128)S(1)}, u32[]{:S(2)}, u32[]{:S(2)}) %collective-permute-start.22) | collective-permute-done | bytes 10272 | tf_op jit(solution)/shard_map/ppermute | solution.py:32
  151.1 1.9 collective-permute-start.24
  153.0 5.6 %collective-permute-start.25 = (f32[1,8,256]{2,1,0:T(8,128)S(1)}, f32[1,8,256]{2,1,0:T(8,128)S(1)}, u32[]{:S(2)}, u32[]{:S(2)}) collective-permute-start(f32[1,8,256]{2,1,0:T(8,128)S(1)} %get-tuple-element.79), channel_id=1, source_target_pairs={{0,2},{2,4},{4,6},{6,8},{8,10},{10,12},{12,14},{14,16},{16,18},{18... | collective-permute-start | bytes 24584 | tf_op jit(solution)/shard_map/ppermute | solution.py:31
  159.4 1.4 collective-permute-start.27
  160.8 1.3 collective-permute-start.26
  162.2 3.0 %collective-permute-done.26 = f32[10,1,256]{2,1,0:T(1,128)S(1)} collective-permute-done((f32[10,1,256]{2,1,0:T(1,128)S(1)}, f32[10,1,256]{2,1,0:T(1,128)S(1)}, u32[]{:S(2)}, u32[]{:S(2)}) %collective-permute-start.26) | collective-permute-done | bytes 10272 | tf_op jit(solution)/shard_map/ppermute | solution.py:32
  165.4 1.9 collective-permute-start.28
  167.3 5.6 %collective-permute-start.29 = (f32[1,8,256]{2,1,0:T(8,128)S(1)}, f32[1,8,256]{2,1,0:T(8,128)S(1)}, u32[]{:S(2)}, u32[]{:S(2)}) collective-permute-start(f32[1,8,256]{2,1,0:T(8,128)S(1)} %get-tuple-element.77), channel_id=1, source_target_pairs={{0,2},{2,4},{4,6},{6,8},{8,10},{10,12},{12,14},{14,16},{16,18},{18... | collective-permute-start | bytes 24584 | tf_op jit(solution)/shard_map/ppermute | solution.py:31
  173.7 1.5 collective-permute-start.31
  175.2 1.3 collective-permute-start.30
  177.4 10.7 %scatter_custom_fusion.5 = f32[5,513]{0,1:T(8,128)S(1)} fusion(s32[4096]{0:T(1024)S(1)} %bitcast.155, f32[4096,5]{1,0:T(8,128)S(1)} %copy.91, f32[]{:T(128)} %constant.73.clone.1), kind=kCustom, calls=%fused_computation.30 | custom fusion | bytes 10264 | tf_op jit(solution)/shard_map/scatter | solution.py:184
  188.2 1.9 collective-permute-start.32
  190.1 5.0 %collective-permute-start.33 = (f32[1,8,256]{2,1,0:T(8,128)S(1)}, f32[1,8,256]{2,1,0:T(8,128)S(1)}, u32[]{:S(2)}, u32[]{:S(2)}) collective-permute-start(f32[1,8,256]{2,1,0:T(8,128)S(1)} %get-tuple-element.75), channel_id=1, source_target_pairs={{0,2},{2,4},{4,6},{6,8},{8,10},{10,12},{12,14},{14,16},{16,18},{18... | collective-permute-start | bytes 24584 | tf_op jit(solution)/shard_map/ppermute | solution.py:31
  195.2 1.3 collective-permute-start.47
  196.5 10.7 %scatter_custom_fusion.4 = f32[5,513]{0,1:T(8,128)S(1)} fusion(s32[4096]{0:T(1024)S(1)} %bitcast.154, f32[4096,5]{1,0:T(8,128)S(1)} %copy.91, f32[]{:T(128)} %constant.73.clone.1), kind=kCustom, calls=%fused_computation.32 | custom fusion | bytes 10264 | tf_op jit(solution)/shard_map/scatter | solution.py:184
  207.8 4.3 %collective-permute-start.35 = (f32[10,1,256]{2,1,0:T(1,128)}, f32[10,1,256]{2,1,0:T(1,128)S(1)}, u32[]{:S(2)}, u32[]{:S(2)}) collective-permute-start(f32[10,1,256]{2,1,0:T(1,128)} %get-tuple-element.57), channel_id=1, source_target_pairs={{0,1},{2,3},{4,5},{6,7},{8,9},{10,11},{12,13},{14,15},{16,17},{18,... | collective-permute-start | bytes 30728 | tf_op jit(solution)/shard_map/ppermute | solution.py:31
  212.0 1.3 collective-permute-start.34
  214.1 5.3 %collective-permute-start.46 = (f32[5,1,512]{0,2,1:T(8,128)}, f32[5,1,512]{0,2,1:T(8,128)}, u32[]{:S(2)}, u32[]{:S(2)}) collective-permute-start(f32[5,1,512]{0,2,1:T(8,128)} %slice_bitcast_fusion.6), channel_id=1, source_target_pairs={{0,1},{2,3},{4,5},{6,7},{8,9},{10,11},{12,13},{14,15},{16,17},{18,... | collective-permute-start | bytes 30728 | tf_op jit(solution)/shard_map/ppermute | solution.py:40
  219.3 10.7 %scatter_custom_fusion.3 = f32[5,513]{0,1:T(8,128)S(1)} fusion(s32[4096]{0:T(1024)S(1)} %bitcast.153, f32[4096,5]{1,0:T(8,128)S(1)} %copy.91, f32[]{:T(128)} %constant.73.clone.1), kind=kCustom, calls=%fused_computation.34 | custom fusion | bytes 10264 | tf_op jit(solution)/shard_map/scatter | solution.py:184
  230.8 1.9 collective-permute-start.36
  232.8 6.9 %collective-permute-start.37 = (f32[1,8,256]{2,1,0:T(8,128)S(1)}, f32[1,8,256]{2,1,0:T(8,128)S(1)}, u32[]{:S(2)}, u32[]{:S(2)}) collective-permute-start(f32[1,8,256]{2,1,0:T(8,128)S(1)} %get-tuple-element.73), channel_id=1, source_target_pairs={{0,2},{2,4},{4,6},{6,8},{8,10},{10,12},{12,14},{14,16},{16,18},{18... | collective-permute-start | bytes 24584 | tf_op jit(solution)/shard_map/ppermute | solution.py:31
  240.4 1.9 collective-permute-start.45
  242.3 10.7 %scatter_custom_fusion.2 = f32[5,513]{0,1:T(8,128)S(1)} fusion(s32[4096]{0:T(1024)S(1)} %bitcast.152, f32[4096,5]{1,0:T(8,128)S(1)} %copy.91, f32[]{:T(128)} %constant.73.clone.1), kind=kCustom, calls=%fused_computation.36 | custom fusion | bytes 10264 | tf_op jit(solution)/shard_map/scatter | solution.py:184
  253.0 1.3 collective-permute-start.39
  254.3 1.3 collective-permute-start.38
  255.6 4.4 %collective-permute-start.44 = (f32[5,1,512]{0,2,1:T(8,128)S(1)}, f32[5,1,512]{0,2,1:T(8,128)S(1)}, u32[]{:S(2)}, u32[]{:S(2)}) collective-permute-start(f32[5,1,512]{0,2,1:T(8,128)S(1)} %slice_bitcast_fusion.8), channel_id=1, source_target_pairs={{0,2},{2,4},{4,6},{6,8},{8,10},{10,12},{12,14},{14,16},{16,18},{18... | collective-permute-start | bytes 30728 | tf_op jit(solution)/shard_map/ppermute | solution.py:40
  260.2 4.5 %collective-permute-start.41 = (f32[1,8,256]{2,1,0:T(8,128)S(1)}, f32[1,8,256]{2,1,0:T(8,128)S(1)}, u32[]{:S(2)}, u32[]{:S(2)}) collective-permute-start(f32[1,8,256]{2,1,0:T(8,128)S(1)} %get-tuple-element.71), channel_id=1, source_target_pairs={{0,2},{2,4},{4,6},{6,8},{8,10},{10,12},{12,14},{14,16},{16,18},{18... | collective-permute-start | bytes 24584 | tf_op jit(solution)/shard_map/ppermute | solution.py:31
  264.8 1.9 collective-permute-start.40
  268.6 1.1 copy.96
  270.7 4.2 %collective-permute-start.43 = (f32[10,1,256]{2,1,0:T(1,128)S(1)}, f32[10,1,256]{2,1,0:T(1,128)S(1)}, u32[]{:S(2)}, u32[]{:S(2)}) collective-permute-start(f32[10,1,256]{2,1,0:T(1,128)S(1)} %get-tuple-element.53), channel_id=1, source_target_pairs={{0,1},{2,3},{4,5},{6,7},{8,9},{10,11},{12,13},{14,15},{16,17},{18,... | collective-permute-start | bytes 30728 | tf_op jit(solution)/shard_map/ppermute | solution.py:31
  274.9 1.3 collective-permute-start.42
  276.9 2.4 collective-permute-done.42
  (163 shorter events, 21.7 us)
Async XLA Ops:
  1.6 79.5 %collective-permute-start = (f32[5,2,8,256]{3,2,1,0:T(8,128)S(1)}, f32[5,2,8,256]{3,2,1,0:T(8,128)S(1)}, u32[]{:S(2)}, u32[]{:S(2)}) collective-permute-start(f32[5,2,8,256]{3,2,1,0:T(8,128)S(1)} %get-tuple-element.45), channel_id=1, source_target_pairs={{0,2},{2,4},{4,6},{6,8},{8,10},{10,12},{12,14},{14,16},{16,18},{18... | collective-permute-start | bytes 245768 | tf_op jit(solution)/shard_map/ppermute | solution.py:31
  6.1 75.0 %collective-permute-start.1 = (f32[5,2,8,256]{3,2,1,0:T(8,128)S(1)}, f32[5,2,8,256]{3,2,1,0:T(8,128)S(1)}, u32[]{:S(2)}, u32[]{:S(2)}) collective-permute-start(f32[5,2,8,256]{3,2,1,0:T(8,128)S(1)} %get-tuple-element.44), channel_id=1, source_target_pairs={{2,0},{4,2},{6,4},{8,6},{10,8},{12,10},{14,12},{16,14},{18,16},{20... | collective-permute-start | bytes 245768 | tf_op jit(solution)/shard_map/ppermute | solution.py:32
  8.8 72.2 %collective-permute-start.5 = (f32[1,8,256]{2,1,0:T(8,128)S(1)}, f32[1,8,256]{2,1,0:T(8,128)S(1)}, u32[]{:S(2)}, u32[]{:S(2)}) collective-permute-start(f32[1,8,256]{2,1,0:T(8,128)S(1)} %get-tuple-element.88), channel_id=1, source_target_pairs={{0,2},{2,4},{4,6},{6,8},{8,10},{10,12},{12,14},{14,16},{16,18},{18... | collective-permute-start | bytes 24584 | tf_op jit(solution)/shard_map/ppermute | solution.py:31
  12.4 7.9 %copy-start.6 = (s32[1,4096]{1,0:T(1,128)S(1)}, s32[1,4096]{1,0:T(1,128)}, u32[]{:S(2)}) copy-start(s32[1,4096]{1,0:T(1,128)} %param.13) | copy-start | bytes 49156
  12.4 68.6 %collective-permute-start.4 = (f32[1,8,256]{2,1,0:T(8,128)S(1)}, f32[1,8,256]{2,1,0:T(8,128)S(1)}, u32[]{:S(2)}, u32[]{:S(2)}) collective-permute-start(f32[1,8,256]{2,1,0:T(8,128)S(1)} %get-tuple-element.87), channel_id=1, source_target_pairs={{2,0},{4,2},{6,4},{8,6},{10,8},{12,10},{14,12},{16,14},{18,16},{20... | collective-permute-start | bytes 24584 | tf_op jit(solution)/shard_map/ppermute | solution.py:32
  20.3 14.9 %copy-start.3 = (f32[4,1,4096]{2,1,0:T(1,128)S(1)}, f32[4,1,4096]{2,1,0:T(1,128)}, u32[]{:S(2)}) copy-start(f32[4,1,4096]{2,1,0:T(1,128)} %param.11) | copy-start | bytes 196612
  20.3 15.1 %copy-start.5 = (f32[1,4096]{1,0:T(1,128)S(1)}, f32[1,4096]{1,0:T(1,128)}, u32[]{:S(2)}) copy-start(f32[1,4096]{1,0:T(1,128)} %param.12) | copy-start | bytes 49156
  20.3 15.2 %copy-start.4 = (s32[1,4096]{1,0:T(1,128)S(1)}, s32[1,4096]{1,0:T(1,128)}, u32[]{:S(2)}) copy-start(s32[1,4096]{1,0:T(1,128)} %param.14) | copy-start | bytes 49156
  34.5 1.9 copy-start.7
  36.4 26.1 %copy-start.8 = (s32[1,8]{1,0:T(1,128)S(1)}, s32[1,8]{1,0:T(1,128)}, u32[]{:S(2)}) copy-start(s32[1,8]{1,0:T(1,128)} %param.15) | copy-start | bytes 100
  36.4 26.1 %copy-start.9 = (s32[1,8]{1,0:T(1,128)S(1)}, s32[1,8]{1,0:T(1,128)}, u32[]{:S(2)}) copy-start(s32[1,8]{1,0:T(1,128)} %param.16) | copy-start | bytes 100
  75.7 5.3 %copy-start.2 = (f32[8,8,256]{2,1,0:T(8,128)S(1)}, f32[8,8,256]{2,1,0:T(8,128)}, u32[]{:S(2)}) copy-start(f32[8,8,256]{2,1,0:T(8,128)} %param.10) | copy-start | bytes 196612
  75.7 5.4 %copy-start = (f32[5,8,8,256]{3,2,1,0:T(8,128)S(1)}, f32[5,8,8,256]{3,2,1,0:T(8,128)}, u32[]{:S(2)}) copy-start(f32[5,8,8,256]{3,2,1,0:T(8,128)} %param.9) | copy-start | bytes 983044
  81.2 7.9 %collective-permute-start.3 = (f32[5,12,2,256]{3,2,1,0:T(2,128)S(1)}, f32[5,12,2,256]{3,2,1,0:T(2,128)S(1)}, u32[]{:S(2)}, u32[]{:S(2)}) collective-permute-start(f32[5,12,2,256]{3,2,1,0:T(2,128)S(1)} %get-tuple-element.41), channel_id=1, source_target_pairs={{1,0},{3,2},{5,4},{7,6},{9,8},{11,10},{13,12},{15,14},{17,16},{19,... | collective-permute-start | bytes 368648 | tf_op jit(solution)/shard_map/ppermute | solution.py:32
  82.5 6.6 %collective-permute-start.2 = (f32[5,12,2,256]{3,2,1,0:T(2,128)S(1)}, f32[5,12,2,256]{3,2,1,0:T(2,128)S(1)}, u32[]{:S(2)}, u32[]{:S(2)}) collective-permute-start(f32[5,12,2,256]{3,2,1,0:T(2,128)S(1)} %get-tuple-element.40), channel_id=1, source_target_pairs={{0,1},{2,3},{4,5},{6,7},{8,9},{10,11},{12,13},{14,15},{16,17},{18,... | collective-permute-start | bytes 368648 | tf_op jit(solution)/shard_map/ppermute | solution.py:31
  86.6 19.4 %collective-permute-start.7 = (f32[10,1,256]{2,1,0:T(1,128)S(1)}, f32[10,1,256]{2,1,0:T(1,128)S(1)}, u32[]{:S(2)}, u32[]{:S(2)}) collective-permute-start(f32[10,1,256]{2,1,0:T(1,128)S(1)} %get-tuple-element.69), channel_id=1, source_target_pairs={{0,1},{2,3},{4,5},{6,7},{8,9},{10,11},{12,13},{14,15},{16,17},{18,... | collective-permute-start | bytes 30728 | tf_op jit(solution)/shard_map/ppermute | solution.py:31
  87.9 18.2 %collective-permute-start.6 = (f32[10,1,256]{2,1,0:T(1,128)S(1)}, f32[10,1,256]{2,1,0:T(1,128)S(1)}, u32[]{:S(2)}, u32[]{:S(2)}) collective-permute-start(f32[10,1,256]{2,1,0:T(1,128)S(1)} %get-tuple-element.68), channel_id=1, source_target_pairs={{1,0},{3,2},{5,4},{7,6},{9,8},{11,10},{13,12},{15,14},{17,16},{19,... | collective-permute-start | bytes 30728 | tf_op jit(solution)/shard_map/ppermute | solution.py:32
  91.9 6.9 %collective-permute-start.9 = (f32[2,1,8,256]{3,2,1,0:T(8,128)S(1)}, f32[2,1,8,256]{3,2,1,0:T(8,128)S(1)}, u32[]{:S(2)}, u32[]{:S(2)}) collective-permute-start(f32[2,1,8,256]{3,2,1,0:T(8,128)S(1)} %get-tuple-element.49), channel_id=1, source_target_pairs={{2,0},{4,2},{6,4},{8,6},{10,8},{12,10},{14,12},{16,14},{18,16},{20... | collective-permute-start | bytes 49160 | tf_op jit(solution)/shard_map/ppermute | solution.py:32
  93.8 5.8 %collective-permute-start.8 = (f32[2,1,8,256]{3,2,1,0:T(8,128)S(1)}, f32[2,1,8,256]{3,2,1,0:T(8,128)S(1)}, u32[]{:S(2)}, u32[]{:S(2)}) collective-permute-start(f32[2,1,8,256]{3,2,1,0:T(8,128)S(1)} %get-tuple-element.48), channel_id=1, source_target_pairs={{0,2},{2,4},{4,6},{6,8},{8,10},{10,12},{12,14},{14,16},{16,18},{18... | collective-permute-start | bytes 49160 | tf_op jit(solution)/shard_map/ppermute | solution.py:31
  99.6 5.4 %collective-permute-start.11 = (f32[2,10,1,256]{3,2,1,0:T(1,128)S(1)}, f32[2,10,1,256]{3,2,1,0:T(1,128)S(1)}, u32[]{:S(2)}, u32[]{:S(2)}) collective-permute-start(f32[2,10,1,256]{3,2,1,0:T(1,128)S(1)} %get-tuple-element.47), channel_id=1, source_target_pairs={{1,0},{3,2},{5,4},{7,6},{9,8},{11,10},{13,12},{15,14},{17,16},{19,... | collective-permute-start | bytes 61448 | tf_op jit(solution)/shard_map/ppermute | solution.py:32
  100.9 5.0 %collective-permute-start.10 = (f32[2,10,1,256]{3,2,1,0:T(1,128)S(1)}, f32[2,10,1,256]{3,2,1,0:T(1,128)S(1)}, u32[]{:S(2)}, u32[]{:S(2)}) collective-permute-start(f32[2,10,1,256]{3,2,1,0:T(1,128)S(1)} %get-tuple-element.46), channel_id=1, source_target_pairs={{0,1},{2,3},{4,5},{6,7},{8,9},{10,11},{12,13},{14,15},{16,17},{18,... | collective-permute-start | bytes 61448 | tf_op jit(solution)/shard_map/ppermute | solution.py:31
  106.2 7.6 %collective-permute-start.12 = (f32[1,8,256]{2,1,0:T(8,128)S(1)}, f32[1,8,256]{2,1,0:T(8,128)S(1)}, u32[]{:S(2)}, u32[]{:S(2)}) collective-permute-start(f32[1,8,256]{2,1,0:T(8,128)S(1)} %get-tuple-element.86), channel_id=1, source_target_pairs={{2,0},{4,2},{6,4},{8,6},{10,8},{12,10},{14,12},{16,14},{18,16},{20... | collective-permute-start | bytes 24584 | tf_op jit(solution)/shard_map/ppermute | solution.py:32
  108.1 6.0 %collective-permute-start.13 = (f32[1,8,256]{2,1,0:T(8,128)S(1)}, f32[1,8,256]{2,1,0:T(8,128)S(1)}, u32[]{:S(2)}, u32[]{:S(2)}) collective-permute-start(f32[1,8,256]{2,1,0:T(8,128)S(1)} %get-tuple-element.85), channel_id=1, source_target_pairs={{0,2},{2,4},{4,6},{6,8},{8,10},{10,12},{12,14},{14,16},{16,18},{18... | collective-permute-start | bytes 24584 | tf_op jit(solution)/shard_map/ppermute | solution.py:31
  114.1 5.3 %collective-permute-start.15 = (f32[10,1,256]{2,1,0:T(1,128)S(1)}, f32[10,1,256]{2,1,0:T(1,128)S(1)}, u32[]{:S(2)}, u32[]{:S(2)}) collective-permute-start(f32[10,1,256]{2,1,0:T(1,128)S(1)} %get-tuple-element.67), channel_id=1, source_target_pairs={{0,1},{2,3},{4,5},{6,7},{8,9},{10,11},{12,13},{14,15},{16,17},{18,... | collective-permute-start | bytes 30728 | tf_op jit(solution)/shard_map/ppermute | solution.py:31
  118.1 4.4 %collective-permute-start.14 = (f32[10,1,256]{2,1,0:T(1,128)S(1)}, f32[10,1,256]{2,1,0:T(1,128)S(1)}, u32[]{:S(2)}, u32[]{:S(2)}) collective-permute-start(f32[10,1,256]{2,1,0:T(1,128)S(1)} %get-tuple-element.66), channel_id=1, source_target_pairs={{1,0},{3,2},{5,4},{7,6},{9,8},{11,10},{13,12},{15,14},{17,16},{19,... | collective-permute-start | bytes 30728 | tf_op jit(solution)/shard_map/ppermute | solution.py:32
  122.6 8.1 %collective-permute-start.16 = (f32[1,8,256]{2,1,0:T(8,128)S(1)}, f32[1,8,256]{2,1,0:T(8,128)S(1)}, u32[]{:S(2)}, u32[]{:S(2)}) collective-permute-start(f32[1,8,256]{2,1,0:T(8,128)S(1)} %get-tuple-element.84), channel_id=1, source_target_pairs={{2,0},{4,2},{6,4},{8,6},{10,8},{12,10},{14,12},{16,14},{18,16},{20... | collective-permute-start | bytes 24584 | tf_op jit(solution)/shard_map/ppermute | solution.py:32
  124.5 6.4 %collective-permute-start.17 = (f32[1,8,256]{2,1,0:T(8,128)S(1)}, f32[1,8,256]{2,1,0:T(8,128)S(1)}, u32[]{:S(2)}, u32[]{:S(2)}) collective-permute-start(f32[1,8,256]{2,1,0:T(8,128)S(1)} %get-tuple-element.83), channel_id=1, source_target_pairs={{0,2},{2,4},{4,6},{6,8},{8,10},{10,12},{12,14},{14,16},{16,18},{18... | collective-permute-start | bytes 24584 | tf_op jit(solution)/shard_map/ppermute | solution.py:31
  131.0 2.8 collective-permute-start.19
  132.3 4.4 %collective-permute-start.18 = (f32[10,1,256]{2,1,0:T(1,128)S(1)}, f32[10,1,256]{2,1,0:T(1,128)S(1)}, u32[]{:S(2)}, u32[]{:S(2)}) collective-permute-start(f32[10,1,256]{2,1,0:T(1,128)S(1)} %get-tuple-element.64), channel_id=1, source_target_pairs={{1,0},{3,2},{5,4},{7,6},{9,8},{11,10},{13,12},{15,14},{17,16},{19,... | collective-permute-start | bytes 30728 | tf_op jit(solution)/shard_map/ppermute | solution.py:32
  136.8 8.0 %collective-permute-start.20 = (f32[1,8,256]{2,1,0:T(8,128)S(1)}, f32[1,8,256]{2,1,0:T(8,128)S(1)}, u32[]{:S(2)}, u32[]{:S(2)}) collective-permute-start(f32[1,8,256]{2,1,0:T(8,128)S(1)} %get-tuple-element.82), channel_id=1, source_target_pairs={{2,0},{4,2},{6,4},{8,6},{10,8},{12,10},{14,12},{16,14},{18,16},{20... | collective-permute-start | bytes 24584 | tf_op jit(solution)/shard_map/ppermute | solution.py:32
  138.8 6.4 %collective-permute-start.21 = (f32[1,8,256]{2,1,0:T(8,128)S(1)}, f32[1,8,256]{2,1,0:T(8,128)S(1)}, u32[]{:S(2)}, u32[]{:S(2)}) collective-permute-start(f32[1,8,256]{2,1,0:T(8,128)S(1)} %get-tuple-element.81), channel_id=1, source_target_pairs={{0,2},{2,4},{4,6},{6,8},{8,10},{10,12},{12,14},{14,16},{16,18},{18... | collective-permute-start | bytes 24584 | tf_op jit(solution)/shard_map/ppermute | solution.py:31
  145.2 2.8 collective-permute-start.23
  146.6 4.4 %collective-permute-start.22 = (f32[10,1,256]{2,1,0:T(1,128)S(1)}, f32[10,1,256]{2,1,0:T(1,128)S(1)}, u32[]{:S(2)}, u32[]{:S(2)}) collective-permute-start(f32[10,1,256]{2,1,0:T(1,128)S(1)} %get-tuple-element.62), channel_id=1, source_target_pairs={{1,0},{3,2},{5,4},{7,6},{9,8},{11,10},{13,12},{15,14},{17,16},{19,... | collective-permute-start | bytes 30728 | tf_op jit(solution)/shard_map/ppermute | solution.py:32
  151.1 8.0 %collective-permute-start.24 = (f32[1,8,256]{2,1,0:T(8,128)S(1)}, f32[1,8,256]{2,1,0:T(8,128)S(1)}, u32[]{:S(2)}, u32[]{:S(2)}) collective-permute-start(f32[1,8,256]{2,1,0:T(8,128)S(1)} %get-tuple-element.80), channel_id=1, source_target_pairs={{2,0},{4,2},{6,4},{8,6},{10,8},{12,10},{14,12},{16,14},{18,16},{20... | collective-permute-start | bytes 24584 | tf_op jit(solution)/shard_map/ppermute | solution.py:32
  153.0 6.4 %collective-permute-start.25 = (f32[1,8,256]{2,1,0:T(8,128)S(1)}, f32[1,8,256]{2,1,0:T(8,128)S(1)}, u32[]{:S(2)}, u32[]{:S(2)}) collective-permute-start(f32[1,8,256]{2,1,0:T(8,128)S(1)} %get-tuple-element.79), channel_id=1, source_target_pairs={{0,2},{2,4},{4,6},{6,8},{8,10},{10,12},{12,14},{14,16},{16,18},{18... | collective-permute-start | bytes 24584 | tf_op jit(solution)/shard_map/ppermute | solution.py:31
  159.4 2.8 collective-permute-start.27
  160.8 4.4 %collective-permute-start.26 = (f32[10,1,256]{2,1,0:T(1,128)S(1)}, f32[10,1,256]{2,1,0:T(1,128)S(1)}, u32[]{:S(2)}, u32[]{:S(2)}) collective-permute-start(f32[10,1,256]{2,1,0:T(1,128)S(1)} %get-tuple-element.60), channel_id=1, source_target_pairs={{1,0},{3,2},{5,4},{7,6},{9,8},{11,10},{13,12},{15,14},{17,16},{19,... | collective-permute-start | bytes 30728 | tf_op jit(solution)/shard_map/ppermute | solution.py:32
  165.4 7.6 %collective-permute-start.28 = (f32[1,8,256]{2,1,0:T(8,128)S(1)}, f32[1,8,256]{2,1,0:T(8,128)S(1)}, u32[]{:S(2)}, u32[]{:S(2)}) collective-permute-start(f32[1,8,256]{2,1,0:T(8,128)S(1)} %get-tuple-element.78), channel_id=1, source_target_pairs={{2,0},{4,2},{6,4},{8,6},{10,8},{12,10},{14,12},{16,14},{18,16},{20... | collective-permute-start | bytes 24584 | tf_op jit(solution)/shard_map/ppermute | solution.py:32
  167.3 6.4 %collective-permute-start.29 = (f32[1,8,256]{2,1,0:T(8,128)S(1)}, f32[1,8,256]{2,1,0:T(8,128)S(1)}, u32[]{:S(2)}, u32[]{:S(2)}) collective-permute-start(f32[1,8,256]{2,1,0:T(8,128)S(1)} %get-tuple-element.77), channel_id=1, source_target_pairs={{0,2},{2,4},{4,6},{6,8},{8,10},{10,12},{12,14},{14,16},{16,18},{18... | collective-permute-start | bytes 24584 | tf_op jit(solution)/shard_map/ppermute | solution.py:31
  173.7 14.3 %collective-permute-start.31 = (f32[10,1,256]{2,1,0:T(1,128)S(1)}, f32[10,1,256]{2,1,0:T(1,128)S(1)}, u32[]{:S(2)}, u32[]{:S(2)}) collective-permute-start(f32[10,1,256]{2,1,0:T(1,128)S(1)} %get-tuple-element.59), channel_id=1, source_target_pairs={{0,1},{2,3},{4,5},{6,7},{8,9},{10,11},{12,13},{14,15},{16,17},{18,... | collective-permute-start | bytes 30728 | tf_op jit(solution)/shard_map/ppermute | solution.py:31
  175.2 12.9 %collective-permute-start.30 = (f32[10,1,256]{2,1,0:T(1,128)S(1)}, f32[10,1,256]{2,1,0:T(1,128)S(1)}, u32[]{:S(2)}, u32[]{:S(2)}) collective-permute-start(f32[10,1,256]{2,1,0:T(1,128)S(1)} %get-tuple-element.58), channel_id=1, source_target_pairs={{1,0},{3,2},{5,4},{7,6},{9,8},{11,10},{13,12},{15,14},{17,16},{19,... | collective-permute-start | bytes 30728 | tf_op jit(solution)/shard_map/ppermute | solution.py:32
  188.2 19.0 %collective-permute-start.32 = (f32[1,8,256]{2,1,0:T(8,128)S(1)}, f32[1,8,256]{2,1,0:T(8,128)S(1)}, u32[]{:S(2)}, u32[]{:S(2)}) collective-permute-start(f32[1,8,256]{2,1,0:T(8,128)S(1)} %get-tuple-element.76), channel_id=1, source_target_pairs={{2,0},{4,2},{6,4},{8,6},{10,8},{12,10},{14,12},{16,14},{18,16},{20... | collective-permute-start | bytes 24584 | tf_op jit(solution)/shard_map/ppermute | solution.py:32
  190.1 17.0 %collective-permute-start.33 = (f32[1,8,256]{2,1,0:T(8,128)S(1)}, f32[1,8,256]{2,1,0:T(8,128)S(1)}, u32[]{:S(2)}, u32[]{:S(2)}) collective-permute-start(f32[1,8,256]{2,1,0:T(8,128)S(1)} %get-tuple-element.75), channel_id=1, source_target_pairs={{0,2},{2,4},{4,6},{6,8},{8,10},{10,12},{12,14},{14,16},{16,18},{18... | collective-permute-start | bytes 24584 | tf_op jit(solution)/shard_map/ppermute | solution.py:31
  195.2 69.6 %collective-permute-start.47 = (f32[5,1,512]{0,2,1:T(8,128)S(1)}, f32[5,1,512]{0,2,1:T(8,128)S(1)}, u32[]{:S(2)}, u32[]{:S(2)}) collective-permute-start(f32[5,1,512]{0,2,1:T(8,128)S(1)} %slice_bitcast_fusion.5), channel_id=1, source_target_pairs={{1,0},{3,2},{5,4},{7,6},{9,8},{11,10},{13,12},{15,14},{17,16},{19,... | collective-permute-start | bytes 30728 | tf_op jit(solution)/shard_map/ppermute | solution.py:40
  207.8 22.2 %collective-permute-start.35 = (f32[10,1,256]{2,1,0:T(1,128)}, f32[10,1,256]{2,1,0:T(1,128)S(1)}, u32[]{:S(2)}, u32[]{:S(2)}) collective-permute-start(f32[10,1,256]{2,1,0:T(1,128)} %get-tuple-element.57), channel_id=1, source_target_pairs={{0,1},{2,3},{4,5},{6,7},{8,9},{10,11},{12,13},{14,15},{16,17},{18,... | collective-permute-start | bytes 30728 | tf_op jit(solution)/shard_map/ppermute | solution.py:31
  212.0 18.0 %collective-permute-start.34 = (f32[10,1,256]{2,1,0:T(1,128)}, f32[10,1,256]{2,1,0:T(1,128)}, u32[]{:S(2)}, u32[]{:S(2)}) collective-permute-start(f32[10,1,256]{2,1,0:T(1,128)} %get-tuple-element.56), channel_id=1, source_target_pairs={{1,0},{3,2},{5,4},{7,6},{9,8},{11,10},{13,12},{15,14},{17,16},{19,... | collective-permute-start | bytes 30728 | tf_op jit(solution)/shard_map/ppermute | solution.py:32
  214.1 53.4 %collective-permute-start.46 = (f32[5,1,512]{0,2,1:T(8,128)}, f32[5,1,512]{0,2,1:T(8,128)}, u32[]{:S(2)}, u32[]{:S(2)}) collective-permute-start(f32[5,1,512]{0,2,1:T(8,128)} %slice_bitcast_fusion.6), channel_id=1, source_target_pairs={{0,1},{2,3},{4,5},{6,7},{8,9},{10,11},{12,13},{14,15},{16,17},{18,... | collective-permute-start | bytes 30728 | tf_op jit(solution)/shard_map/ppermute | solution.py:40
  230.8 22.1 %collective-permute-start.36 = (f32[1,8,256]{2,1,0:T(8,128)S(1)}, f32[1,8,256]{2,1,0:T(8,128)S(1)}, u32[]{:S(2)}, u32[]{:S(2)}) collective-permute-start(f32[1,8,256]{2,1,0:T(8,128)S(1)} %get-tuple-element.74), channel_id=1, source_target_pairs={{2,0},{4,2},{6,4},{8,6},{10,8},{12,10},{14,12},{16,14},{18,16},{20... | collective-permute-start | bytes 24584 | tf_op jit(solution)/shard_map/ppermute | solution.py:32
  232.8 20.2 %collective-permute-start.37 = (f32[1,8,256]{2,1,0:T(8,128)S(1)}, f32[1,8,256]{2,1,0:T(8,128)S(1)}, u32[]{:S(2)}, u32[]{:S(2)}) collective-permute-start(f32[1,8,256]{2,1,0:T(8,128)S(1)} %get-tuple-element.73), channel_id=1, source_target_pairs={{0,2},{2,4},{4,6},{6,8},{8,10},{10,12},{12,14},{14,16},{16,18},{18... | collective-permute-start | bytes 24584 | tf_op jit(solution)/shard_map/ppermute | solution.py:31
  240.4 28.2 %collective-permute-start.45 = (f32[5,1,512]{0,2,1:T(8,128)}, f32[5,1,512]{0,2,1:T(8,128)}, u32[]{:S(2)}, u32[]{:S(2)}) collective-permute-start(f32[5,1,512]{0,2,1:T(8,128)} %slice_bitcast_fusion.7), channel_id=1, source_target_pairs={{2,0},{4,2},{6,4},{8,6},{10,8},{12,10},{14,12},{16,14},{18,16},{20... | collective-permute-start | bytes 30728 | tf_op jit(solution)/shard_map/ppermute | solution.py:40
  253.0 2.6 collective-permute-start.39
  254.3 5.8 %collective-permute-start.38 = (f32[10,1,256]{2,1,0:T(1,128)S(1)}, f32[10,1,256]{2,1,0:T(1,128)S(1)}, u32[]{:S(2)}, u32[]{:S(2)}) collective-permute-start(f32[10,1,256]{2,1,0:T(1,128)S(1)} %get-tuple-element.54), channel_id=1, source_target_pairs={{1,0},{3,2},{5,4},{7,6},{9,8},{11,10},{13,12},{15,14},{17,16},{19,... | collective-permute-start | bytes 30728 | tf_op jit(solution)/shard_map/ppermute | solution.py:32
  255.6 14.0 %collective-permute-start.44 = (f32[5,1,512]{0,2,1:T(8,128)S(1)}, f32[5,1,512]{0,2,1:T(8,128)S(1)}, u32[]{:S(2)}, u32[]{:S(2)}) collective-permute-start(f32[5,1,512]{0,2,1:T(8,128)S(1)} %slice_bitcast_fusion.8), channel_id=1, source_target_pairs={{0,2},{2,4},{4,6},{6,8},{8,10},{10,12},{12,14},{14,16},{16,18},{18... | collective-permute-start | bytes 30728 | tf_op jit(solution)/shard_map/ppermute | solution.py:40
  260.2 20.0 %copy-start.1 = (f32[8,8,256]{2,1,0:T(8,128)}, f32[8,8,256]{2,1,0:T(8,128)S(1)}, u32[]{:S(2)}) copy-start(f32[8,8,256]{2,1,0:T(8,128)S(1)} %fusion.45) | copy-start | bytes 196612
  260.2 9.6 %collective-permute-start.41 = (f32[1,8,256]{2,1,0:T(8,128)S(1)}, f32[1,8,256]{2,1,0:T(8,128)S(1)}, u32[]{:S(2)}, u32[]{:S(2)}) collective-permute-start(f32[1,8,256]{2,1,0:T(8,128)S(1)} %get-tuple-element.71), channel_id=1, source_target_pairs={{0,2},{2,4},{4,6},{6,8},{8,10},{10,12},{12,14},{14,16},{16,18},{18... | collective-permute-start | bytes 24584 | tf_op jit(solution)/shard_map/ppermute | solution.py:31
  264.8 5.9 %collective-permute-start.40 = (f32[1,8,256]{2,1,0:T(8,128)S(1)}, f32[1,8,256]{2,1,0:T(8,128)S(1)}, u32[]{:S(2)}, u32[]{:S(2)}) collective-permute-start(f32[1,8,256]{2,1,0:T(8,128)S(1)} %get-tuple-element.72), channel_id=1, source_target_pairs={{2,0},{4,2},{6,4},{8,6},{10,8},{12,10},{14,12},{16,14},{18,16},{20... | collective-permute-start | bytes 24584 | tf_op jit(solution)/shard_map/ppermute | solution.py:32
  270.7 6.3 %collective-permute-start.43 = (f32[10,1,256]{2,1,0:T(1,128)S(1)}, f32[10,1,256]{2,1,0:T(1,128)S(1)}, u32[]{:S(2)}, u32[]{:S(2)}) collective-permute-start(f32[10,1,256]{2,1,0:T(1,128)S(1)} %get-tuple-element.53), channel_id=1, source_target_pairs={{0,1},{2,3},{4,5},{6,7},{8,9},{10,11},{12,13},{14,15},{16,17},{18,... | collective-permute-start | bytes 30728 | tf_op jit(solution)/shard_map/ppermute | solution.py:31
  274.9 4.4 %collective-permute-start.42 = (f32[10,1,256]{2,1,0:T(1,128)S(1)}, f32[10,1,256]{2,1,0:T(1,128)S(1)}, u32[]{:S(2)}, u32[]{:S(2)}) collective-permute-start(f32[10,1,256]{2,1,0:T(1,128)S(1)} %get-tuple-element.52), channel_id=1, source_target_pairs={{1,0},{3,2},{5,4},{7,6},{9,8},{11,10},{13,12},{15,14},{17,16},{19,... | collective-permute-start | bytes 30728 | tf_op jit(solution)/shard_map/ppermute | solution.py:32
where the time goes:
time: 283 us; the launch traced here: 280 us
  starting transfers between devices  134 us (47%)
  local copies, waits for them, and re-layouts  77.4 us (27%)
  other arithmetic  48.1 us (17%)
  waiting for transfers between devices  18.9 us (7%)
    ppermute x22, starting transfers between devices, padded_2(): before = lax.ppermute(last, axis, up)  85.9 us
    scatter x4, local copies, waits for them, and re-layouts, body(): parcel = jnp.zeros((5, CAP + 1), jnp.float32).at[:, place].set(renewed)  42.6 us
    ppermute x22, starting transfers between devices, padded_2(): after = lax.ppermute(leading, axis, down)  35.3 us
    scatter-add x1, other arithmetic, body(): sources = jnp.zeros((3, volume), jnp.float32).at[:, cells].add(drop_sources)  26.1 us
    ppermute x22, waiting for transfers between devices, padded_2(): after = lax.ppermute(leading, axis, down)  15.3 us
    gather x2, local copies, waits for them, and re-layouts, body(): local = flat[:, cells]  14.8 us
    ppermute x4, starting transfers between devices, shifted(): return lax.ppermute(shard, axis, pairs)  12.9 us
    scatter-add x1, other arithmetic, body(): sources.at[:, spray_cell[0]].add(spray(spray_on[0], spray_time[0]))  7.24 us
  transfers between devices with their start and end apart: 48, of which 13 were waited for; matrix products, arithmetic and copies ran while one was open for 44% of the time, Pallas kernels for 0%

commit v1 on v0

v1 whole, which is shorter than its diff:
```python
import functools

import jax
import jax.numpy as jnp
from jax import lax
from jax.experimental import pallas as pl
from jax.experimental.pallas import tpu as pltpu
from jax.sharding import PartitionSpec as P

ITERS = 8
TIME_STEP = 0.2
DIFFUSION = 0.1
DRAG_TIME = 0.5
HEAT_TIME = 1.0
GRAVITY = 1.0
VAPOUR_RATE = 0.5
DRAG_COUPLING = 0.5
LATENT = 2.0
SPRAY_RATE = 3.0
CLOCK = 100.0
SPRAY_RAMP = 50.0

MESH = pl.DeviceIdType.MESH
F32 = jnp.float32
BF16 = jnp.bfloat16
CHUNK = 1024
NT = (((1,), (1,)), ((), ()))
SIDES = ((1, 0), (-1, 0), (0, 1), (0, -1))
AROUND = SIDES + ((1, 1), (1, -1), (-1, 1), (-1, -1))


def split(values):
    high = values.astype(BF16).astype(F32)
    return high, values - high


def droplet_kernel(
    gas, motion, size, cell, target, spray_on, spray_time, spray_cell,
    sources, parcels, kept, grid_pieces, summed, packed,
):
    slots = size.shape[1]
    rows = gas.shape[1] * gas.shape[2]
    depth = gas.shape[3]
    table = gas[0:4].reshape(4 * rows, depth)
    high, low = split(table)
    grid_pieces[...] = jnp.concatenate([high, low], axis=0).astype(BF16)
    summed[...] = jnp.zeros_like(summed)
    packed[...] = jnp.zeros_like(packed)
    upper = (
        lax.broadcasted_iota(jnp.int32, (256, 256), 0) <= lax.broadcasted_iota(jnp.int32, (256, 256), 1)
    ).astype(F32).astype(BF16)
    eight = lax.broadcasted_iota(jnp.int32, (8, 256), 0)

    def step(turn, carry):
        here = pl.ds(pl.multiple_of(turn * CHUNK, CHUNK), CHUNK)
        cells = cell[:, here]
        goal = target[:, here]
        diameter = size[:, here]
        moving = motion[:, 0, here]
        at_z = jnp.bitwise_and(cells, depth - 1)
        at_xy = lax.shift_right_logical(cells, depth.bit_length() - 1)
        hot_z = (lax.broadcasted_iota(jnp.int32, (depth, CHUNK), 0) == at_z).astype(F32).astype(BF16)
        in_xy = lax.broadcasted_iota(jnp.int32, (rows, CHUNK), 0) == at_xy
        hot_xy = in_xy.astype(F32)
        found = jnp.dot(grid_pieces[...], hot_z, preferred_element_type=F32)
        found = found[: 4 * rows] + found[4 * rows :]
        local = jnp.concatenate(
            [jnp.sum(found[f * rows : (f + 1) * rows] * hot_xy, axis=0, keepdims=True) for f in range(4)], axis=0
        )
        gap = local - moving
        field = lax.broadcasted_iota(jnp.int32, gap.shape, 0)
        pace = jnp.where(field == 3, TIME_STEP / HEAT_TIME, TIME_STEP / DRAG_TIME)
        fall = jnp.where(field == 2, TIME_STEP * GRAVITY, 0.0)
        carried = moving + pace * gap - fall
        vapour = VAPOUR_RATE * diameter * (1.0 / (1.0 + jnp.exp(-gap[3:4])))
        shrunk = diameter - TIME_STEP * vapour
        renewed = jnp.concatenate([carried, shrunk], axis=0)
        kept[:, 0, here] = jnp.where(goal == 4, renewed, 0.0)
        alive = goal >= 0
        drag = jnp.where(alive, -DRAG_COUPLING * diameter * diameter * gap[2:3], 0.0)
        vapour = jnp.where(alive, vapour, 0.0)
        drag_high, drag_low = split(drag)
        vapour_high, vapour_low = split(vapour)
        spread = jnp.concatenate(
            [hot_xy * drag_high, hot_xy * vapour_high, hot_xy * drag_low, hot_xy * vapour_low], axis=0
        ).astype(BF16)
        summed[...] += lax.dot_general(spread, hot_z, NT, preferred_element_type=F32)

        pieces = [(eight == goal[:, k * 256 : k * 256 + 256]).astype(F32) for k in range(CHUNK // 256)]
        counts = jnp.dot(jnp.concatenate(pieces, axis=0).astype(BF16), upper, preferred_element_type=F32)
        places = []
        for k, piece in enumerate(pieces):
            count = counts[8 * k : 8 * k + 8] + carry
            carry = count[:, 255:256]
            place = jnp.where(eight < 4, piece * (count + (512.0 * eight.astype(F32))), 0.0)
            places.append(jnp.sum(place, axis=0, keepdims=True))
        place = jnp.concatenate(places, axis=1).astype(jnp.int32) - 1
        hot_low = (
            lax.broadcasted_iota(jnp.int32, (256, CHUNK), 0) == jnp.bitwise_and(place, 255)
        ).astype(F32).astype(BF16)
        hot_high = (
            lax.broadcasted_iota(jnp.int32, (8, CHUNK), 0) == lax.shift_right_arithmetic(place, 8)
        ).astype(F32)
        top, rest = split(renewed)
        bundle = jnp.concatenate(
            [hot_high * top[f : f + 1] for f in range(5)] + [hot_high * rest[f : f + 1] for f in range(5)], axis=0
        ).astype(BF16)
        packed[...] += lax.dot_general(bundle, hot_low, NT, preferred_element_type=F32)
        return carry

    lax.fori_loop(0, slots // CHUNK, step, jnp.zeros((8, 1), F32))

    numbers = lax.broadcasted_iota(jnp.int32, (rows, depth), 0) * depth + lax.broadcasted_iota(
        jnp.int32, (rows, depth), 1
    )
    ramp = jnp.clip((CLOCK - spray_time[...].astype(F32)) / SPRAY_RAMP, 0.0, 1.0)
    strength = SPRAY_RATE * ramp * spray_on[...].astype(F32)
    spray = jnp.zeros((rows, depth), F32)
    for head in range(spray_on.shape[1]):
        spray += jnp.where(numbers == spray_cell[:, head : head + 1], strength[:, head : head + 1], 0.0)
    total = summed[...]
    drag = total[:rows] + total[2 * rows : 3 * rows]
    vapour = total[rows : 2 * rows] + total[3 * rows :]
    shape = gas.shape[1:]
    sources[0] = (TIME_STEP * (drag - spray)).reshape(shape)
    sources[1] = (TIME_STEP * (-LATENT * vapour - spray)).reshape(shape)
    sources[2] = (TIME_STEP * vapour).reshape(shape)
    bundle = packed[0:40] + packed[40:80]
    parcels[...] = jnp.zeros_like(parcels)
    for f in range(5):
        for way in range(4):
            for half in range(2):
                row = f * 8 + 2 * way + half
                parcels[way, f : f + 1, half * 256 : half * 256 + 256] = bundle[row : row + 1]


def flow_kernel(
    n_gx, n_gy,
    gas, guess, sources, parcels,
    gas_next, pressure, arrived,
    wide, tall, edge_send, edge_recv, around, region, swap, star, tall_v, u_halo, v_send, v_recv, landed,
    send_halo, recv_halo, send_star, recv_star, send_parcel, recv_parcel, send_sum, recv_sum, send_src, recv_src,
):
    me_x, me_y = lax.axis_index("gx"), lax.axis_index("gy")

    def exists(dx, dy):
        to_x, to_y = me_x + dx, me_y + dy
        return (to_x >= 0) & (to_x < n_gx) & (to_y >= 0) & (to_y < n_gy)

    def device(dx, dy):
        return {"gx": jnp.clip(me_x + dx, 0, n_gx - 1), "gy": jnp.clip(me_y + dy, 0, n_gy - 1)}

    def copy(src, dst, send, recv, spot, side):
        return pltpu.make_async_remote_copy(
            src_ref=src, dst_ref=dst, send_sem=send.at[spot], recv_sem=recv.at[spot],
            device_id=device(*side), device_id_type=MESH,
        )

    def start(copies, sides):
        for one, (dx, dy) in zip(copies, sides):
            pl.when(exists(dx, dy))(one.start)

    def receive(copies, sides):
        for one, (dx, dy) in zip(copies, sides):
            pl.when(exists(-dx, -dy))(one.wait_recv)

    def sent(copies, sides):
        for one, (dx, dy) in zip(copies, sides):
            pl.when(exists(dx, dy))(one.wait_send)

    barrier = pltpu.get_barrier_semaphore()
    for dx, dy in AROUND:
        @pl.when(exists(dx, dy))
        def _():
            pl.semaphore_signal(barrier, inc=1, device_id=device(dx, dy), device_id_type=MESH)

    wide[0:5, 2:10] = gas[...]
    wide[5, 2:10] = guess[...]
    for f in range(6):
        own = guess[...] if f == 5 else gas[f]
        tall[f, :, 8:16] = own
        edge_send[0, f] = own[:, 6:8]
        edge_send[1, f] = own[:, 0:2]

    @pl.when(~exists(-1, 0))
    def _():
        wide[:, 0:2] = jnp.zeros((6, 2, 8, 256), F32)
        u_halo[0] = jnp.zeros((8, 256), F32)

    @pl.when(~exists(1, 0))
    def _():
        wide[:, 10:12] = jnp.zeros((6, 2, 8, 256), F32)
        u_halo[1] = jnp.zeros((8, 256), F32)

    @pl.when(~exists(0, -1))
    def _():
        edge_recv[0] = jnp.zeros((6, 8, 2, 256), F32)
        v_recv[0] = jnp.zeros((8, 1, 256), F32)

    @pl.when(~exists(0, 1))
    def _():
        edge_recv[1] = jnp.zeros((6, 8, 2, 256), F32)
        v_recv[1] = jnp.zeros((8, 1, 256), F32)

    for way, (dx, dy) in enumerate(SIDES):
        @pl.when(~exists(-dx, -dy))
        def _():
            landed[way] = jnp.zeros((8, 512), F32)

    for dx, dy in AROUND:
        @pl.when(~exists(dx, dy))
        def _():
            spot = (pl.ds(8 + 8 * dx, 8), pl.ds(8 + 8 * dy, 8))
            around[spot] = jnp.zeros((8, 8, 256), F32)
            region[spot] = jnp.zeros((8, 8, 256), F32)

    pl.semaphore_wait(barrier, sum(exists(dx, dy).astype(jnp.int32) for dx, dy in AROUND))

    halo = [
        copy(wide.at[:, pl.ds(8, 2)], wide.at[:, pl.ds(0, 2)], send_halo, recv_halo, 0, SIDES[0]),
        copy(wide.at[:, pl.ds(2, 2)], wide.at[:, pl.ds(10, 2)], send_halo, recv_halo, 1, SIDES[1]),
        copy(edge_send.at[0], edge_recv.at[0], send_halo, recv_halo, 2, SIDES[2]),
        copy(edge_send.at[1], edge_recv.at[1], send_halo, recv_halo, 3, SIDES[3]),
    ]
    start(halo, SIDES)
    parcel = [
        copy(parcels.at[way], landed.at[way], send_parcel, recv_parcel, way, SIDES[way]) for way in range(4)
    ]
    start(parcel, SIDES)
    receive(halo, SIDES)

    along = lax.broadcasted_iota(jnp.int32, (1, 1, 256), 2)
    masks = {
        1: (along >= 1).astype(F32), 2: (along >= 2).astype(F32),
        -1: (along < 255).astype(F32), -2: (along < 254).astype(F32),
    }

    def below(values, by):
        return pltpu.roll(values, by % 256, 2) * masks[by]

    for f in range(6):
        tall[f, :, 6:8] = edge_recv[0, f]
        tall[f, :, 16:18] = edge_recv[1, f]

    pace = [gas[0], gas[1], gas[2]]
    for f in (0, 1, 2, 3, 4):
        centre = gas[f]
        near_x, near_x2 = wide[f, 3:11], wide[f, 1:9]
        near_y, near_y2 = tall[f, :, 9:17], tall[f, :, 7:15]
        near_z, near_z2 = below(centre, -1), below(centre, 1)
        laplace = near_x + near_x2 + near_y + near_y2 + near_z + near_z2 - 6.0 * centre
        slope_x = 8.0 * (near_x - near_x2) - (wide[f, 4:12] - wide[f, 0:8])
        slope_y = 8.0 * (near_y - near_y2) - (tall[f, :, 10:18] - tall[f, :, 6:14])
        slope_z = 8.0 * (near_z - near_z2) - (below(centre, -2) - below(centre, 2))
        transport = (pace[0] * slope_x + pace[1] * slope_y + pace[2] * slope_z) * (1.0 / 12.0)
        result = centre + TIME_STEP * (DIFFUSION * laplace - transport)
        if f >= 2:
            result = result + sources[f - 2]
        star[f] = result

    tall_v[:, 8:16] = star[1]
    v_send[0] = star[1, :, 7:8]
    v_send[1] = star[1, :, 0:1]
    edges = [
        copy(star.at[0, 7], u_halo.at[0], send_star, recv_star, 0, SIDES[0]),
        copy(star.at[0, 0], u_halo.at[1], send_star, recv_star, 1, SIDES[1]),
        copy(v_send.at[0], v_recv.at[0], send_star, recv_star, 2, SIDES[2]),
        copy(v_send.at[1], v_recv.at[1], send_star, recv_star, 3, SIDES[3]),
    ]
    start(edges, SIDES)

    own = (pl.ds(8, 8), pl.ds(8, 8))
    around[own] = (
        wide[5, 3:11] + wide[5, 1:9] + tall[5, :, 9:17] + tall[5, :, 7:15]
        + below(guess[...], 1) + below(guess[...], -1)
    )

    def blocks(buffer, send, recv):
        return [
            copy(
                buffer.at[own], buffer.at[pl.ds(8 - 8 * dx, 8), pl.ds(8 - 8 * dy, 8)],
                send, recv, spot, (dx, dy),
            )
            for spot, (dx, dy) in enumerate(AROUND)
        ]

    sums = blocks(around, send_sum, recv_sum)
    start(sums, AROUND)
    receive(edges, SIDES)
    tall_v[:, 7:8] = v_recv[0]
    tall_v[:, 16:17] = v_recv[1]
    speed = star[0]
    spread_x = jnp.concatenate([speed[1:8], u_halo[1:2]], axis=0) - jnp.concatenate(
        [u_halo[0:1], speed[0:7]], axis=0
    )
    lift = star[2]
    spread = spread_x + (tall_v[:, 9:17] - tall_v[:, 7:15]) + (below(lift, -1) - below(lift, 1))
    region[own] = spread * (0.5 / TIME_STEP)
    parts = blocks(region, send_src, recv_src)
    start(parts, AROUND)

    receive(parcel, SIDES)
    for way in range(4):
        arrived[way, :, 0, :] = landed[way, 0:5]

    receive(sums, AROUND)
    receive(parts, AROUND)

    row = lax.broadcasted_iota(jnp.int32, (1, 24, 256), 1)
    low_y, high_y = exists(0, -1).astype(F32), exists(0, 1).astype(F32)
    factor = jnp.where(row < 8, low_y, jnp.where(row < 16, 1.0, high_y)) * (1.0 / 6.0)
    factors = [factor * exists(-1, 0).astype(F32), factor, factor * exists(1, 0).astype(F32)]

    for x in range(0, 24, 4):
        swap[0, x : x + 4] = (around[x : x + 4] - region[x : x + 4]) * factors[x // 8]
    for turn in range(1, ITERS):
        old, new = swap.at[(turn - 1) % 2], swap.at[turn % 2]
        x = turn
        while x < 24 - turn:
            end = min(x + 4, 24 - turn, (x // 8 + 1) * 8)
            centre = old[x:end]
            total = old[x - 1 : end - 1] + old[x + 1 : end + 1]
            total = total + pltpu.roll(centre, 1, 1) + pltpu.roll(centre, 23, 1)
            total = total + below(centre, 1) + below(centre, -1)
            new[x:end] = (total - region[x:end]) * factors[x // 8]
            x = end

    last = swap.at[(ITERS - 1) % 2]
    final = last[8:16, 8:16]
    pressure[...] = final
    half = TIME_STEP * 0.5
    gas_next[0] = star[0] - half * (last[9:17, 8:16] - last[7:15, 8:16])
    gas_next[1] = star[1] - half * (last[8:16, 9:17] - last[8:16, 7:15])
    gas_next[2] = star[2] - half * (below(final, -1) - below(final, 1))
    gas_next[3] = star[3]
    gas_next[4] = star[4]

    sent(halo, SIDES)
    sent(parcel, SIDES)
    sent(edges, SIDES)
    sent(sums, AROUND)
    sent(parts, AROUND)


def body(
    n_gx, n_gy,
    gas_state, pressure_guess, drop_motion, drop_size, drop_cell, drop_target, spray_on, spray_time, spray_cell,
):
    vmem = pl.BlockSpec(memory_space=pltpu.VMEM)
    slots = drop_size.shape[1]
    block = gas_state.shape[1:]
    sources, parcels, kept = pl.pallas_call(
        droplet_kernel,
        out_shape=(
            jax.ShapeDtypeStruct((3,) + block, F32),
            jax.ShapeDtypeStruct((4, 8, 512), F32),
            jax.ShapeDtypeStruct((5, 1, slots), F32),
        ),
        in_specs=[vmem] * 8,
        out_specs=(vmem,) * 3,
        scratch_shapes=[
            pltpu.VMEM((512, 256), BF16),
            pltpu.VMEM((256, 256), F32),
            pltpu.VMEM((80, 256), F32),
        ],
        compiler_params=pltpu.CompilerParams(vmem_limit_bytes=40 * 1024 * 1024),
    )(gas_state, drop_motion, drop_size, drop_cell, drop_target, spray_on, spray_time, spray_cell)
    dma = pltpu.SemaphoreType.DMA
    gas_next, pressure, arrived = pl.pallas_call(
        functools.partial(flow_kernel, n_gx, n_gy),
        out_shape=(
            jax.ShapeDtypeStruct(gas_state.shape, F32),
            jax.ShapeDtypeStruct(block, F32),
            jax.ShapeDtypeStruct((4, 5, 1, 512), F32),
        ),
        in_specs=[vmem] * 4,
        out_specs=(vmem,) * 3,
        scratch_shapes=[
            pltpu.VMEM((6, 12, 8, 256), F32),
            pltpu.VMEM((6, 8, 24, 256), F32),
            pltpu.VMEM((2, 6, 8, 2, 256), F32),
            pltpu.VMEM((2, 6, 8, 2, 256), F32),
            pltpu.VMEM((24, 24, 256), F32),
            pltpu.VMEM((24, 24, 256), F32),
            pltpu.VMEM((2, 24, 24, 256), F32),
            pltpu.VMEM((5, 8, 8, 256), F32),
            pltpu.VMEM((8, 24, 256), F32),
            pltpu.VMEM((2, 8, 256), F32),
            pltpu.VMEM((2, 8, 1, 256), F32),
            pltpu.VMEM((2, 8, 1, 256), F32),
            pltpu.VMEM((4, 8, 512), F32),
        ]
        + [dma((4,))] * 6 + [dma((8,))] * 4,
        compiler_params=pltpu.CompilerParams(
            collective_id=0, has_side_effects=True, vmem_limit_bytes=40 * 1024 * 1024
        ),
    )(gas_state, pressure_guess, sources, parcels)
    return gas_next, pressure, kept, arrived


def solution(mesh):
    in_specs = (
        P(None, "gx", "gy", None),
        P("gx", "gy", None),
        P(None, "gx", "gy"),
    ) + (P("gx", "gy"),) * 6
    out_specs = (
        P(None, "gx", "gy", None),
        P("gx", "gy", None),
        P(None, "gx", "gy"),
        P(None, None, "gx", "gy"),
    )
    inner = functools.partial(body, mesh.shape["gx"], mesh.shape["gy"])
    return jax.shard_map(inner, mesh=mesh, in_specs=in_specs, out_specs=out_specs, check_vma=False)
```

time: 283 us -> 35.8 us (0.13)
  the two profiles are of different devices: /device:TPU:1 before, /device:TPU:0 now
where the time goes in v1:
time: 35.8 us; the launch traced here: 35.4 us
  Pallas kernels  26.8 us (75%)
  local copies, waits for them, and re-layouts  7.9 us (22%)
  between operations  0.67 us (2%)
    pallas_call x1, Pallas kernels, body(): pl.pallas_call(functools.partial(flow_kernel, n_gx, n_gy), out_shape=(jax...  21.3 us
    unnamed x21, local copies, waits for them, and re-layouts  7.9 us
    pallas_call x1, Pallas kernels, body(): pl.pallas_call(droplet_kernel, out_shape=(jax.ShapeDtypeStruct((3,) + blo...  5.51 us

profile of v1, /device:TPU:0, one launch (start us, length us, event | category | flops | bytes accessed | tf_op | source)
XLA Modules:
  0.0 35.4 jit_solution(9267894131256447661)
XLA Ops:
  0.6 0.0 copy-start
  0.6 1.0 %copy-done = f32[5,8,8,256]{3,2,1,0:T(8,128)S(1)} copy-done((f32[5,8,8,256]{3,2,1,0:T(8,128)S(1)}, f32[5,8,8,256]{3,2,1,0:T(8,128)}, u32[]{:S(2)}) %copy-start) | copy-done | bytes 327704
  1.6 0.0 copy-start.2
  1.6 0.8 %copy-done.2 = f32[4,1,4096]{2,1,0:T(1,128)S(1)} copy-done((f32[4,1,4096]{2,1,0:T(1,128)S(1)}, f32[4,1,4096]{2,1,0:T(1,128)}, u32[]{:S(2)}) %copy-start.2) | copy-done | bytes 65560
  2.4 0.0 copy-start.3
  2.4 0.7 %copy-done.3 = f32[1,4096]{1,0:T(1,128)S(1)} copy-done((f32[1,4096]{1,0:T(1,128)S(1)}, f32[1,4096]{1,0:T(1,128)}, u32[]{:S(2)}) %copy-start.3) | copy-done | bytes 16408
  3.2 0.0 copy-start.4
  3.2 0.7 %copy-done.4 = s32[1,4096]{1,0:T(1,128)S(1)} copy-done((s32[1,4096]{1,0:T(1,128)S(1)}, s32[1,4096]{1,0:T(1,128)}, u32[]{:S(2)}) %copy-start.4) | copy-done | bytes 16408
  3.9 0.0 copy-start.5
  3.9 0.7 %copy-done.5 = s32[1,4096]{1,0:T(1,128)S(1)} copy-done((s32[1,4096]{1,0:T(1,128)S(1)}, s32[1,4096]{1,0:T(1,128)}, u32[]{:S(2)}) %copy-start.5) | copy-done | bytes 16408
  4.6 0.0 copy-start.6
  4.6 0.7 %copy-done.6 = s32[1,8]{1,0:T(1,128)S(1)} copy-done((s32[1,8]{1,0:T(1,128)S(1)}, s32[1,8]{1,0:T(1,128)}, u32[]{:S(2)}) %copy-start.6) | copy-done | bytes 56
  5.3 0.0 copy-start.7
  5.3 0.7 %copy-done.7 = s32[1,8]{1,0:T(1,128)S(1)} copy-done((s32[1,8]{1,0:T(1,128)S(1)}, s32[1,8]{1,0:T(1,128)}, u32[]{:S(2)}) %copy-start.7) | copy-done | bytes 56
  5.9 0.0 copy-start.8
  5.9 0.7 %copy-done.8 = s32[1,8]{1,0:T(1,128)S(1)} copy-done((s32[1,8]{1,0:T(1,128)S(1)}, s32[1,8]{1,0:T(1,128)}, u32[]{:S(2)}) %copy-start.8) | copy-done | bytes 56
  6.6 0.0 copy-start.1
  6.6 5.5 %shard_map.120 = (f32[3,8,8,256]{3,2,1,0:T(8,128)S(1)}, f32[4,8,512]{2,1,0:T(8,128)S(1)}, f32[5,1,4096]{2,1,0:T(1,128)}) custom-call(f32[5,8,8,256]{3,2,1,0:T(8,128)S(1)} %copy-done, f32[4,1,4096]{2,1,0:T(1,128)S(1)} %copy-done.2, f32[1,4096]{1,0:T(1,128)S(1)} %copy-done.3, s32[1,4096]{1,0:T(1,128)S(1)} %copy-done.4, s32[1,4096]{1,0:T(1,128)S(1)} %copy-done.5, ...), custom_call_target="tpu_custom_call" | custom-call | tf_op jit(solution)/shard_map/pallas_call | solution.py:352
  12.1 0.0 copy-done.1
  12.1 21.3 %shard_map.121 = (f32[5,8,8,256]{3,2,1,0:T(8,128)S(1)}, f32[8,8,256]{2,1,0:T(8,128)S(1)}, f32[4,5,1,512]{3,2,1,0:T(1,128)S(1)}) custom-call(f32[5,8,8,256]{3,2,1,0:T(8,128)S(1)} %copy-done, f32[8,8,256]{2,1,0:T(8,128)S(1)} %copy-done.1, f32[3,8,8,256]{3,2,1,0:T(8,128)S(1)} %get-tuple-element.10.sources, f32[4,8,512]{2,1,0:T(8,128)S(1)} %get-tuple-element.11.parcels), custom_call_target="tpu_custom_call" | custom-call | tf_op jit(solution)/shard_map/pallas_call | solution.py:369
  33.4 0.7 %copy.16 = f32[5,8,8,256]{3,2,1,0:T(8,128)} copy(f32[5,8,8,256]{3,2,1,0:T(8,128)S(1)} %get-tuple-element.20) | data formatting | bytes 655360
  34.1 0.6 %copy.17 = f32[8,8,256]{2,1,0:T(8,128)} copy(f32[8,8,256]{2,1,0:T(8,128)S(1)} %get-tuple-element.21) | data formatting | bytes 131072
  34.8 0.6 %copy.18 = f32[4,5,1,512]{3,2,1,0:T(1,128)} copy(f32[4,5,1,512]{3,2,1,0:T(1,128)S(1)} %get-tuple-element.23) | data formatting | bytes 81920
Async XLA Ops:
  0.6 1.0 %copy-start = (f32[5,8,8,256]{3,2,1,0:T(8,128)S(1)}, f32[5,8,8,256]{3,2,1,0:T(8,128)}, u32[]{:S(2)}) copy-start(f32[5,8,8,256]{3,2,1,0:T(8,128)} %gas.3) | copy-start | bytes 983044
  1.6 0.8 %copy-start.2 = (f32[4,1,4096]{2,1,0:T(1,128)S(1)}, f32[4,1,4096]{2,1,0:T(1,128)}, u32[]{:S(2)}) copy-start(f32[4,1,4096]{2,1,0:T(1,128)} %motion.1) | copy-start | bytes 196612
  2.4 0.7 %copy-start.3 = (f32[1,4096]{1,0:T(1,128)S(1)}, f32[1,4096]{1,0:T(1,128)}, u32[]{:S(2)}) copy-start(f32[1,4096]{1,0:T(1,128)} %size.1) | copy-start | bytes 49156
  3.2 0.7 %copy-start.4 = (s32[1,4096]{1,0:T(1,128)S(1)}, s32[1,4096]{1,0:T(1,128)}, u32[]{:S(2)}) copy-start(s32[1,4096]{1,0:T(1,128)} %cell.1) | copy-start | bytes 49156
  3.9 0.7 %copy-start.5 = (s32[1,4096]{1,0:T(1,128)S(1)}, s32[1,4096]{1,0:T(1,128)}, u32[]{:S(2)}) copy-start(s32[1,4096]{1,0:T(1,128)} %target.1) | copy-start | bytes 49156
  4.6 0.7 %copy-start.6 = (s32[1,8]{1,0:T(1,128)S(1)}, s32[1,8]{1,0:T(1,128)}, u32[]{:S(2)}) copy-start(s32[1,8]{1,0:T(1,128)} %spray_on.1) | copy-start | bytes 100
  5.3 0.7 %copy-start.7 = (s32[1,8]{1,0:T(1,128)S(1)}, s32[1,8]{1,0:T(1,128)}, u32[]{:S(2)}) copy-start(s32[1,8]{1,0:T(1,128)} %spray_time.1) | copy-start | bytes 100
  5.9 0.7 %copy-start.8 = (s32[1,8]{1,0:T(1,128)S(1)}, s32[1,8]{1,0:T(1,128)}, u32[]{:S(2)}) copy-start(s32[1,8]{1,0:T(1,128)} %spray_cell.1) | copy-start | bytes 100
  6.6 5.5 %copy-start.1 = (f32[8,8,256]{2,1,0:T(8,128)S(1)}, f32[8,8,256]{2,1,0:T(8,128)}, u32[]{:S(2)}) copy-start(f32[8,8,256]{2,1,0:T(8,128)} %guess.1) | copy-start | bytes 196612

commit v2 on v1

v2 whole, which is shorter than its diff:
```python
import functools

import jax
import jax.numpy as jnp
from jax import lax
from jax.experimental import pallas as pl
from jax.experimental.pallas import tpu as pltpu
from jax.sharding import PartitionSpec as P

ITERS = 8
TIME_STEP = 0.2
DIFFUSION = 0.1
DRAG_TIME = 0.5
HEAT_TIME = 1.0
GRAVITY = 1.0
VAPOUR_RATE = 0.5
DRAG_COUPLING = 0.5
LATENT = 2.0
SPRAY_RATE = 3.0
CLOCK = 100.0
SPRAY_RAMP = 50.0

MESH = pl.DeviceIdType.MESH
F32 = jnp.float32
BF16 = jnp.bfloat16
CHUNK = 1024
NT = (((1,), (1,)), ((), ()))
SIDES = ((1, 0), (-1, 0), (0, 1), (0, -1))
CORNERS = ((1, 1), (1, -1), (-1, 1), (-1, -1))
AROUND = SIDES + CORNERS


def split(values):
    high = values.astype(BF16).astype(F32)
    return high, values - high


def along_depth(values, by):
    place = lax.broadcasted_iota(jnp.int32, (1, 1, 256), 2)
    keep = place >= by if by > 0 else place < 256 + by
    return pltpu.roll(values, by % 256, 2) * keep.astype(F32)


def evolve_kernel(
    n_gx, n_gy,
    gas_hbm, guess_hbm, motion_hbm, size_hbm, cell_hbm, target_hbm, on_hbm, time_hbm, place_hbm,
    gas_next, pressure, kept_hbm, arrived_hbm,
    star, factors, kept, arrived, swap, final,
    motion, size, cell, target, spray_on, spray_time, spray_cell,
    grid_pieces, summed, packed, renewed, parcels, landed,
    wide, tall, edge_send, edge_recv, sums, parts, corner_send, corner_recv, tall_v, u_halo, v_send, v_recv,
    send_in, send_out, send_halo, recv_halo, send_star, recv_star, send_parcel, recv_parcel, send_sum, recv_sum, send_src,
    recv_src,
):
    me_x, me_y = lax.axis_index("gx"), lax.axis_index("gy")
    slots = size.shape[1]
    rows, depth = 64, 256

    def exists(dx, dy):
        to_x, to_y = me_x + dx, me_y + dy
        return (to_x >= 0) & (to_x < n_gx) & (to_y >= 0) & (to_y < n_gy)

    def device(dx, dy):
        return {"gx": jnp.clip(me_x + dx, 0, n_gx - 1), "gy": jnp.clip(me_y + dy, 0, n_gy - 1)}

    def copy(src, dst, send, recv, spot, side):
        return pltpu.make_async_remote_copy(
            src_ref=src, dst_ref=dst, send_sem=send.at[spot], recv_sem=recv.at[spot],
            device_id=device(*side), device_id_type=MESH,
        )

    def start(copies, sides):
        for one, (dx, dy) in zip(copies, sides):
            pl.when(exists(dx, dy))(one.start)

    def receive(copies, sides):
        for one, (dx, dy) in zip(copies, sides):
            pl.when(exists(-dx, -dy))(one.wait_recv)

    def sent(copies, sides):
        for one, (dx, dy) in zip(copies, sides):
            pl.when(exists(dx, dy))(one.wait_send)

    loads = [
        pltpu.make_async_copy(src, dst, send_in.at[spot])
        for spot, (src, dst) in enumerate(
            (
                (gas_hbm, wide.at[pl.ds(0, 5), pl.ds(2, 8)]),
                (guess_hbm, wide.at[5, pl.ds(2, 8)]),
                (gas_hbm, tall.at[pl.ds(0, 5), :, pl.ds(8, 8)]),
                (guess_hbm, tall.at[5, :, pl.ds(8, 8)]),
                (cell_hbm, cell),
                (motion_hbm, motion),
                (size_hbm, size),
                (target_hbm, target),
                (on_hbm, spray_on),
                (time_hbm, spray_time),
                (place_hbm, spray_cell),
            )
        )
    ]
    for one in loads:
        one.start()

    barrier = pltpu.get_barrier_semaphore()
    for dx, dy in AROUND:
        @pl.when(exists(dx, dy))
        def _():
            pl.semaphore_signal(barrier, inc=1, device_id=device(dx, dy), device_id_type=MESH)

    @pl.when(~exists(-1, 0))
    def _():
        wide[:, 0:2] = jnp.zeros((6, 2, 8, 256), F32)
        u_halo[0] = jnp.zeros((8, 256), F32)

    @pl.when(~exists(1, 0))
    def _():
        wide[:, 10:12] = jnp.zeros((6, 2, 8, 256), F32)
        u_halo[1] = jnp.zeros((8, 256), F32)

    @pl.when(~exists(0, -1))
    def _():
        edge_recv[0] = jnp.zeros((6, 8, 2, 256), F32)
        v_recv[0] = jnp.zeros((8, 1, 256), F32)

    @pl.when(~exists(0, 1))
    def _():
        edge_recv[1] = jnp.zeros((6, 8, 2, 256), F32)
        v_recv[1] = jnp.zeros((8, 1, 256), F32)

    for way, (dx, dy) in enumerate(SIDES):
        @pl.when(~exists(-dx, -dy))
        def _():
            spot = (pl.ds(8 - 8 * dx, 8), pl.ds(8 - 8 * dy, 8))
            landed[way] = jnp.zeros((8, 512), F32)
            sums[spot] = jnp.zeros((8, 8, 256), F32)
            parts[spot] = jnp.zeros((8, 8, 256), F32)

    for way, (dx, dy) in enumerate(CORNERS):
        @pl.when(~exists(-dx, -dy))
        def _():
            corner_recv[0, way] = jnp.zeros((4, 8, 256), F32)
            corner_recv[1, way] = jnp.zeros((4, 8, 256), F32)

    row = lax.broadcasted_iota(jnp.int32, (24, 256), 0)
    low_y, high_y = exists(0, -1).astype(F32), exists(0, 1).astype(F32)
    factor = jnp.where(row < 8, low_y, jnp.where(row < 16, 1.0, high_y)) * (1.0 / 6.0)
    factors[0] = factor * exists(-1, 0).astype(F32)
    factors[1] = factor
    factors[2] = factor * exists(1, 0).astype(F32)
    summed[...] = jnp.zeros_like(summed)
    packed[...] = jnp.zeros_like(packed)

    for one in loads[0:4]:
        one.wait()
    for f in range(6):
        own = wide[f, 2:10]
        edge_send[0, f] = own[:, 6:8]
        edge_send[1, f] = own[:, 0:2]
    pl.semaphore_wait(barrier, sum(exists(dx, dy).astype(jnp.int32) for dx, dy in AROUND))
    halo = [
        copy(wide.at[:, pl.ds(8, 2)], wide.at[:, pl.ds(0, 2)], send_halo, recv_halo, 0, SIDES[0]),
        copy(wide.at[:, pl.ds(2, 2)], wide.at[:, pl.ds(10, 2)], send_halo, recv_halo, 1, SIDES[1]),
        copy(edge_send.at[0], edge_recv.at[0], send_halo, recv_halo, 2, SIDES[2]),
        copy(edge_send.at[1], edge_recv.at[1], send_halo, recv_halo, 3, SIDES[3]),
    ]
    start(halo, SIDES)

    high, low = split(wide[0:4, 2:10].reshape(4 * rows, depth))
    grid_pieces[...] = jnp.concatenate([high, low], axis=0).astype(BF16)
    for one in loads[4:]:
        one.wait()

    def exchange(turn, carry):
        here = pl.ds(pl.multiple_of(turn * CHUNK, CHUNK), CHUNK)
        cells = cell[:, here]
        goal = target[:, here]
        diameter = size[:, here]
        moving = motion[:, 0, here]
        at_z = jnp.bitwise_and(cells, depth - 1)
        at_xy = lax.shift_right_logical(cells, 8)
        hot_z = (lax.broadcasted_iota(jnp.int32, (depth, CHUNK), 0) == at_z).astype(F32).astype(BF16)
        hot_xy = (lax.broadcasted_iota(jnp.int32, (rows, CHUNK), 0) == at_xy).astype(F32)
        found = jnp.dot(grid_pieces[...], hot_z, preferred_element_type=F32)
        found = found[: 4 * rows] + found[4 * rows :]
        local = jnp.concatenate(
            [jnp.sum(found[f * rows : (f + 1) * rows] * hot_xy, axis=0, keepdims=True) for f in range(4)], axis=0
        )
        gap = local - moving
        field = lax.broadcasted_iota(jnp.int32, gap.shape, 0)
        pace = jnp.where(field == 3, TIME_STEP / HEAT_TIME, TIME_STEP / DRAG_TIME)
        fall = jnp.where(field == 2, TIME_STEP * GRAVITY, 0.0)
        carried = moving + pace * gap - fall
        vapour = VAPOUR_RATE * diameter * (1.0 / (1.0 + jnp.exp(-gap[3:4])))
        fresh = jnp.concatenate([carried, diameter - TIME_STEP * vapour], axis=0)
        renewed[0:5, here] = fresh
        kept[:, 0, here] = jnp.where(goal == 4, fresh, 0.0)
        alive = goal >= 0
        drag = jnp.where(alive, -DRAG_COUPLING * diameter * diameter * gap[2:3], 0.0)
        vapour = jnp.where(alive, vapour, 0.0)
        drag_high, drag_low = split(drag)
        vapour_high, vapour_low = split(vapour)
        spread = jnp.concatenate(
            [hot_xy * drag_high, hot_xy * vapour_high, hot_xy * drag_low, hot_xy * vapour_low], axis=0
        ).astype(BF16)
        summed[...] += lax.dot_general(spread, hot_z, NT, preferred_element_type=F32)
        return carry

    turns = slots // CHUNK
    lax.fori_loop(0, turns // 2, exchange, 0)

    receive(halo, SIDES)
    for f in range(6):
        tall[f, :, 6:8] = edge_recv[0, f]
        tall[f, :, 16:18] = edge_recv[1, f]
    for f in range(5):
        centre = wide[f, 2:10]
        near_x, near_x2 = wide[f, 3:11], wide[f, 1:9]
        near_y, near_y2 = tall[f, :, 9:17], tall[f, :, 7:15]
        near_z, near_z2 = along_depth(centre, -1), along_depth(centre, 1)
        laplace = near_x + near_x2 + near_y + near_y2 + near_z + near_z2 - 6.0 * centre
        slope_x = 8.0 * (near_x - near_x2) - (wide[f, 4:12] - wide[f, 0:8])
        slope_y = 8.0 * (near_y - near_y2) - (tall[f, :, 10:18] - tall[f, :, 6:14])
        slope_z = 8.0 * (near_z - near_z2) - (along_depth(centre, -2) - along_depth(centre, 2))
        transport = (wide[0, 2:10] * slope_x + wide[1, 2:10] * slope_y + wide[2, 2:10] * slope_z) * (1.0 / 12.0)
        star[f] = centre + TIME_STEP * (DIFFUSION * laplace - transport)
        if f == 1:
            tall_v[:, 8:16] = star[1]
            v_send[0] = star[1, :, 7:8]
            v_send[1] = star[1, :, 0:1]
            u_halo[2] = star[0, 7]
            u_halo[3] = star[0, 0]
            edges = [
                copy(u_halo.at[2], u_halo.at[0], send_star, recv_star, 0, SIDES[0]),
                copy(u_halo.at[3], u_halo.at[1], send_star, recv_star, 1, SIDES[1]),
                copy(v_send.at[0], v_recv.at[0], send_star, recv_star, 2, SIDES[2]),
                copy(v_send.at[1], v_recv.at[1], send_star, recv_star, 3, SIDES[3]),
            ]
            start(edges, SIDES)

    own = (pl.ds(8, 8), pl.ds(8, 8))
    tile_row = lax.broadcasted_iota(jnp.int32, (8, 256), 0)

    def layer(dx, i):
        return 8 - i if dx > 0 else i - 1

    def blocks(buffer, which, send, recv):
        block = buffer[own]
        for way, (dx, dy) in enumerate(CORNERS):
            for i in range(1, 5):
                near, far = block[layer(dx, i)], block[layer(dx, 9 - i)]
                if i > 1:
                    if dy > 0:
                        near = jnp.where(tile_row >= i, near, pltpu.roll(far, i - 1, 0))
                    else:
                        near = jnp.where(tile_row < 8 - i, near, pltpu.roll(far, 9 - i, 0))
                corner_send[which, way, i - 1] = near
        copies = [
            copy(
                buffer.at[own], buffer.at[pl.ds(8 - 8 * dx, 8), pl.ds(8 - 8 * dy, 8)],
                send, recv, spot, (dx, dy),
            )
            for spot, (dx, dy) in enumerate(SIDES)
        ]
        copies += [
            copy(corner_send.at[which, way], corner_recv.at[which, way], send, recv, 4 + way, side)
            for way, side in enumerate(CORNERS)
        ]
        start(copies, AROUND)
        return copies

    def unpack(buffer, which):
        for way, (dx, dy) in enumerate(CORNERS):
            base, side = 8 - 8 * dx, slice(8 - 8 * dy, 16 - 8 * dy)
            for i in range(1, 5):
                tile = corner_recv[which, way, i - 1]
                buffer[base + layer(dx, i), side] = tile
                back = (9 - i if dy > 0 else i - 1) % 8
                buffer[base + layer(dx, 9 - i), side] = pltpu.roll(tile, back, 0) if back else tile

    sums[own] = (
        wide[5, 3:11] + wide[5, 1:9] + tall[5, :, 9:17] + tall[5, :, 7:15]
        + along_depth(wide[5, 2:10], 1) + along_depth(wide[5, 2:10], -1)
    )
    sum_copies = blocks(sums, 0, send_sum, recv_sum)

    lax.fori_loop(turns // 2, turns, exchange, 0)

    numbers = lax.broadcasted_iota(jnp.int32, (rows, depth), 0) * depth + lax.broadcasted_iota(
        jnp.int32, (rows, depth), 1
    )
    ramp = jnp.clip((CLOCK - spray_time[...].astype(F32)) / SPRAY_RAMP, 0.0, 1.0)
    strength = SPRAY_RATE * ramp * spray_on[...].astype(F32)
    spray = jnp.zeros((rows, depth), F32)
    for head in range(spray_on.shape[1]):
        spray += jnp.where(numbers == spray_cell[:, head : head + 1], strength[:, head : head + 1], 0.0)
    total = summed[...]
    drag = total[:rows] + total[2 * rows : 3 * rows]
    vapour = total[rows : 2 * rows] + total[3 * rows :]
    lift = star[2] + (TIME_STEP * (drag - spray)).reshape(8, 8, 256)
    star[2] = lift

    receive(edges, SIDES)
    tall_v[:, 7:8] = v_recv[0]
    tall_v[:, 16:17] = v_recv[1]
    speed = star[0]
    spread_x = jnp.concatenate([speed[1:8], u_halo[1:2]], axis=0) - jnp.concatenate(
        [u_halo[0:1], speed[0:7]], axis=0
    )
    spread = spread_x + (tall_v[:, 9:17] - tall_v[:, 7:15]) + (along_depth(lift, -1) - along_depth(lift, 1))
    parts[own] = spread * (0.5 / TIME_STEP)
    part_copies = blocks(parts, 1, send_src, recv_src)

    star[3] = star[3] + (TIME_STEP * (-LATENT * vapour - spray)).reshape(8, 8, 256)
    star[4] = star[4] + (TIME_STEP * vapour).reshape(8, 8, 256)

    early = [
        pltpu.make_async_copy(star.at[pl.ds(3, 2)], gas_next.at[pl.ds(3, 2)], send_out.at[0]),
        pltpu.make_async_copy(kept, kept_hbm, send_out.at[1]),
    ]
    for one in early:
        one.start()

    upper = (
        lax.broadcasted_iota(jnp.int32, (256, 256), 0) <= lax.broadcasted_iota(jnp.int32, (256, 256), 1)
    ).astype(F32).astype(BF16)
    eight = lax.broadcasted_iota(jnp.int32, (8, 256), 0)

    def pack(turn, carry):
        here = pl.ds(pl.multiple_of(turn * CHUNK, CHUNK), CHUNK)
        goal = target[:, here]
        pieces = [(eight == goal[:, k * 256 : k * 256 + 256]).astype(F32) for k in range(CHUNK // 256)]
        counts = jnp.dot(jnp.concatenate(pieces, axis=0).astype(BF16), upper, preferred_element_type=F32)
        places = []
        for k, piece in enumerate(pieces):
            count = counts[8 * k : 8 * k + 8] + carry
            carry = count[:, 255:256]
            place = jnp.where(eight < 4, piece * (count + (512.0 * eight.astype(F32))), 0.0)
            places.append(jnp.sum(place, axis=0, keepdims=True))
        place = jnp.concatenate(places, axis=1).astype(jnp.int32) - 1
        hot_low = (
            lax.broadcasted_iota(jnp.int32, (256, CHUNK), 0) == jnp.bitwise_and(place, 255)
        ).astype(F32).astype(BF16)
        hot_high = (
            lax.broadcasted_iota(jnp.int32, (8, CHUNK), 0) == lax.shift_right_arithmetic(place, 8)
        ).astype(F32)
        top, rest = split(renewed[0:5, here])
        bundle = jnp.concatenate(
            [hot_high * top[f : f + 1] for f in range(5)] + [hot_high * rest[f : f + 1] for f in range(5)], axis=0
        ).astype(BF16)
        packed[...] += lax.dot_general(bundle, hot_low, NT, preferred_element_type=F32)
        return carry

    lax.fori_loop(0, turns, pack, jnp.zeros((8, 1), F32))
    bundle = packed[0:40] + packed[40:80]
    for f in range(5):
        for way in range(4):
            for half in range(2):
                spot = f * 8 + 2 * way + half
                parcels[way, f : f + 1, half * 256 : half * 256 + 256] = bundle[spot : spot + 1]
    for way in range(4):
        parcels[way, 5:8] = jnp.zeros((3, 512), F32)
    parcel = [
        copy(parcels.at[way], landed.at[way], send_parcel, recv_parcel, way, SIDES[way]) for way in range(4)
    ]
    start(parcel, SIDES)

    receive(sum_copies, AROUND)
    unpack(sums, 0)
    receive(part_copies, AROUND)
    unpack(parts, 1)

    for x in range(0, 24, 4):
        swap[0, x : x + 4] = (sums[x : x + 4] - parts[x : x + 4]) * factors[x // 8]
    for turn in range(1, ITERS):
        old, new = swap.at[(turn - 1) % 2], swap.at[turn % 2]
        x = turn
        while x < 24 - turn:
            end = min(x + 4, 24 - turn, (x // 8 + 1) * 8)
            centre = old[x:end]
            total = old[x - 1 : end - 1] + old[x + 1 : end + 1]
            total = total + pltpu.roll(centre, 1, 1) + pltpu.roll(centre, 23, 1)
            total = total + along_depth(centre, 1) + along_depth(centre, -1)
            new[x:end] = (total - parts[x:end]) * factors[x // 8]
            x = end

    last = swap.at[(ITERS - 1) % 2]
    centre = last[8:16, 8:16]
    final[...] = centre
    half = TIME_STEP * 0.5
    star[0] = star[0] - half * (last[9:17, 8:16] - last[7:15, 8:16])
    star[1] = star[1] - half * (last[8:16, 9:17] - last[8:16, 7:15])
    star[2] = star[2] - half * (along_depth(centre, -1) - along_depth(centre, 1))
    late = [
        pltpu.make_async_copy(star.at[pl.ds(0, 3)], gas_next.at[pl.ds(0, 3)], send_out.at[2]),
        pltpu.make_async_copy(final, pressure, send_out.at[3]),
    ]
    for one in late:
        one.start()
    receive(parcel, SIDES)
    for way in range(4):
        arrived[way, :, 0, :] = landed[way, 0:5]
    late.append(pltpu.make_async_copy(arrived, arrived_hbm, send_out.at[4]))
    late[2].start()

    sent(halo, SIDES)
    sent(edges, SIDES)
    sent(sum_copies, AROUND)
    sent(part_copies, AROUND)
    sent(parcel, SIDES)
    for one in early + late:
        one.wait()


def hand_over_kernel(*refs):
    sems = refs[-1]
    copies = [pltpu.make_async_copy(refs[k], refs[4 + k], sems.at[k]) for k in range(4)]
    for one in copies:
        one.start()
    for one in copies:
        one.wait()


def body(
    n_gx, n_gy,
    gas_state, pressure_guess, drop_motion, drop_size, drop_cell, drop_target, spray_on, spray_time, spray_cell,
):
    hbm = pl.BlockSpec(memory_space=pltpu.HBM)
    dma = pltpu.SemaphoreType.DMA
    slots = drop_size.shape[1]
    heads = spray_on.shape[1]
    block = gas_state.shape[1:]
    shape = functools.partial(jax.ShapeDtypeStruct, dtype=F32)
    outs = (shape(gas_state.shape), shape(block), shape((5, 1, slots)), shape((4, 5, 1, 512)))
    results = pl.pallas_call(
        functools.partial(evolve_kernel, n_gx, n_gy),
        out_shape=outs,
        in_specs=[hbm] * 9,
        out_specs=(hbm,) * 4,
        scratch_shapes=[
            pltpu.VMEM(gas_state.shape, F32),
            pltpu.VMEM((3, 24, 256), F32),
            pltpu.VMEM((5, 1, slots), F32),
            pltpu.VMEM((4, 5, 1, 512), F32),
            pltpu.VMEM((2, 24, 24, 256), F32),
            pltpu.VMEM(block, F32),
            pltpu.VMEM(drop_motion.shape, F32),
            pltpu.VMEM((1, slots), F32),
            pltpu.VMEM((1, slots), jnp.int32),
            pltpu.VMEM((1, slots), jnp.int32),
            pltpu.VMEM((1, heads), jnp.int32),
            pltpu.VMEM((1, heads), jnp.int32),
            pltpu.VMEM((1, heads), jnp.int32),
            pltpu.VMEM((512, 256), BF16),
            pltpu.VMEM((256, 256), F32),
            pltpu.VMEM((80, 256), F32),
            pltpu.VMEM((8, slots), F32),
            pltpu.VMEM((4, 8, 512), F32),
            pltpu.VMEM((4, 8, 512), F32),
            pltpu.VMEM((6, 12, 8, 256), F32),
            pltpu.VMEM((6, 8, 24, 256), F32),
            pltpu.VMEM((2, 6, 8, 2, 256), F32),
            pltpu.VMEM((2, 6, 8, 2, 256), F32),
            pltpu.VMEM((24, 24, 256), F32),
            pltpu.VMEM((24, 24, 256), F32),
            pltpu.VMEM((2, 4, 4, 8, 256), F32),
            pltpu.VMEM((2, 4, 4, 8, 256), F32),
            pltpu.VMEM((8, 24, 256), F32),
            pltpu.VMEM((4, 8, 256), F32),
            pltpu.VMEM((2, 8, 1, 256), F32),
            pltpu.VMEM((2, 8, 1, 256), F32),
        ]
        + [dma((11,)), dma((5,))] + [dma((4,))] * 6 + [dma((8,))] * 4,
        compiler_params=pltpu.CompilerParams(
            collective_id=0, has_side_effects=True, vmem_limit_bytes=60 * 1024 * 1024
        ),
    )(
        gas_state, pressure_guess, drop_motion, drop_size, drop_cell, drop_target, spray_on, spray_time, spray_cell
    )
    return pl.pallas_call(
        hand_over_kernel,
        out_shape=outs,
        in_specs=[hbm] * 4,
        out_specs=(hbm,) * 4,
        scratch_shapes=[dma((4,))],
        compiler_params=pltpu.CompilerParams(vmem_limit_bytes=60 * 1024 * 1024),
    )(*results)


def solution(mesh):
    in_specs = (
        P(None, "gx", "gy", None),
        P("gx", "gy", None),
        P(None, "gx", "gy"),
    ) + (P("gx", "gy"),) * 6
    out_specs = (
        P(None, "gx", "gy", None),
        P("gx", "gy", None),
        P(None, "gx", "gy"),
        P(None, None, "gx", "gy"),
    )
    inner = functools.partial(body, mesh.shape["gx"], mesh.shape["gy"])
    return jax.shard_map(inner, mesh=mesh, in_specs=in_specs, out_specs=out_specs, check_vma=False)
```

time: 35.8 us -> 36.9 us (1.031)
  the two profiles are of different devices: /device:TPU:0 before, /device:TPU:1 now
where the time goes in v2:
time: 36.9 us; the launch traced here: 36.7 us
  Pallas kernels  36.1 us (98%)
  between operations  0.64 us (2%)
    pallas_call x1, Pallas kernels, body(): pl.pallas_call(functools.partial(evolve_kernel, n_gx, n_gy), out_shape=ou...  19.3 us
    pallas_call x1, Pallas kernels, body(): pl.pallas_call(hand_over_kernel, out_shape=outs, in_specs=[hbm] * 4, out_...  16.8 us

profile of v2, /device:TPU:1, one launch (start us, length us, event | category | flops | bytes accessed | tf_op | source)
XLA Modules:
  0.0 36.7 jit_solution(15924601674264351525)
XLA Ops:
  0.6 19.3 %shard_map.120 = (f32[5,8,8,256]{3,2,1,0:T(8,128)}, f32[8,8,256]{2,1,0:T(8,128)}, f32[5,1,4096]{2,1,0:T(1,128)}, f32[4,5,1,512]{3,2,1,0:T(1,128)}) custom-call(f32[5,8,8,256]{3,2,1,0:T(8,128)} %gas_hbm.1, f32[8,8,256]{2,1,0:T(8,128)} %guess_hbm.1, f32[4,1,4096]{2,1,0:T(1,128)} %motion_hbm.1, f32[1,4096]{1,0:T(1,128)} %size_hbm.1, s32[1,4096]{1,0:T(1,128)} %cell_hbm.1, ...), custom_call_target="tpu_custom_call" | custom-call | tf_op jit(solution)/shard_map/pallas_call | solution.py:435
  19.9 16.8 %shard_map.121 = (f32[5,8,8,256]{3,2,1,0:T(8,128)}, f32[8,8,256]{2,1,0:T(8,128)}, f32[5,1,4096]{2,1,0:T(1,128)}, f32[4,5,1,512]{3,2,1,0:T(1,128)}) custom-call(f32[5,8,8,256]{3,2,1,0:T(8,128)} %get-tuple-element.8.refs_0_, f32[8,8,256]{2,1,0:T(8,128)} %get-tuple-element.9.refs_1_, f32[5,1,4096]{2,1,0:T(1,128)} %get-tuple-element.10.refs_2_, ...), custom_call_target="tpu_custom_call" | custom-call | tf_op jit(solution)/shard_map/pallas_call | solution.py:480

commit v3 on v2

--- a/solution.py
+++ b/solution.py
@@ -36,9 +36,15 @@
 
 
 def along_depth(values, by):
-    place = lax.broadcasted_iota(jnp.int32, (1, 1, 256), 2)
-    keep = place >= by if by > 0 else place < 256 + by
-    return pltpu.roll(values, by % 256, 2) * keep.astype(F32)
+    lane = lax.broadcasted_iota(jnp.int32, (1, 1, 128), 2)
+    first = pltpu.roll(values[:, :, :128], by % 128, 2)
+    second = pltpu.roll(values[:, :, 128:], by % 128, 2)
+    if by > 0:
+        return jnp.concatenate(
+            [jnp.where(lane < by, 0.0, first), jnp.where(lane < by, first, second)], axis=2
+        )
+    inside = lane < 128 + by
+    return jnp.concatenate([jnp.where(inside, first, second), jnp.where(inside, second, 0.0)], axis=2)
 
 
 def evolve_kernel(
@@ -48,8 +54,8 @@
     star, factors, kept, arrived, swap, final,
     motion, size, cell, target, spray_on, spray_time, spray_cell,
     grid_pieces, summed, packed, renewed, parcels, landed,
-    wide, tall, edge_send, edge_recv, sums, parts, corner_send, corner_recv, tall_v, u_halo, v_send, v_recv,
-    send_in, send_out, send_halo, recv_halo, send_star, recv_star, send_parcel, recv_parcel, send_sum, recv_sum, send_src,
+    guess, rim, side_send, side_recv, wide, tall, edge_send, edge_recv, sums, parts, corner_send, corner_recv, tall_v, u_halo, v_send, v_recv,
+    send_in, send_out, send_rim, recv_rim, send_halo, recv_halo, send_star, recv_star, send_parcel, recv_parcel, send_sum, recv_sum, send_src,
     recv_src,
 ):
     me_x, me_y = lax.axis_index("gx"), lax.axis_index("gy")
@@ -85,10 +91,10 @@
         pltpu.make_async_copy(src, dst, send_in.at[spot])
         for spot, (src, dst) in enumerate(
             (
-                (gas_hbm, wide.at[pl.ds(0, 5), pl.ds(2, 8)]),
-                (guess_hbm, wide.at[5, pl.ds(2, 8)]),
-                (gas_hbm, tall.at[pl.ds(0, 5), :, pl.ds(8, 8)]),
-                (guess_hbm, tall.at[5, :, pl.ds(8, 8)]),
+                (guess_hbm, rim.at[pl.ds(1, 8)]),
+                (guess_hbm, guess.at[:, pl.ds(8, 8)]),
+                (gas_hbm, wide.at[:, pl.ds(2, 8)]),
+                (gas_hbm, tall.at[:, :, pl.ds(8, 8)]),
                 (cell_hbm, cell),
                 (motion_hbm, motion),
                 (size_hbm, size),
@@ -110,22 +116,26 @@
 
     @pl.when(~exists(-1, 0))
     def _():
-        wide[:, 0:2] = jnp.zeros((6, 2, 8, 256), F32)
+        wide[:, 0:2] = jnp.zeros((5, 2, 8, 256), F32)
+        rim[0] = jnp.zeros((8, 256), F32)
         u_halo[0] = jnp.zeros((8, 256), F32)
 
     @pl.when(~exists(1, 0))
     def _():
-        wide[:, 10:12] = jnp.zeros((6, 2, 8, 256), F32)
+        wide[:, 10:12] = jnp.zeros((5, 2, 8, 256), F32)
+        rim[9] = jnp.zeros((8, 256), F32)
         u_halo[1] = jnp.zeros((8, 256), F32)
 
     @pl.when(~exists(0, -1))
     def _():
-        edge_recv[0] = jnp.zeros((6, 8, 2, 256), F32)
+        edge_recv[0] = jnp.zeros((5, 8, 2, 256), F32)
+        side_recv[0] = jnp.zeros((8, 1, 256), F32)
         v_recv[0] = jnp.zeros((8, 1, 256), F32)
 
     @pl.when(~exists(0, 1))
     def _():
-        edge_recv[1] = jnp.zeros((6, 8, 2, 256), F32)
+        edge_recv[1] = jnp.zeros((5, 8, 2, 256), F32)
+        side_recv[1] = jnp.zeros((8, 1, 256), F32)
         v_recv[1] = jnp.zeros((8, 1, 256), F32)
 
     for way, (dx, dy) in enumerate(SIDES):
@@ -153,11 +163,20 @@
 
     for one in loads[0:4]:
         one.wait()
-    for f in range(6):
+    side_send[0] = rim[1:9, 7:8]
+    side_send[1] = rim[1:9, 0:1]
+    for f in range(5):
         own = wide[f, 2:10]
         edge_send[0, f] = own[:, 6:8]
         edge_send[1, f] = own[:, 0:2]
     pl.semaphore_wait(barrier, sum(exists(dx, dy).astype(jnp.int32) for dx, dy in AROUND))
+    border = [
+        copy(rim.at[8], rim.at[0], send_rim, recv_rim, 0, SIDES[0]),
+        copy(rim.at[1], rim.at[9], send_rim, recv_rim, 1, SIDES[1]),
+        copy(side_send.at[0], side_recv.at[0], send_rim, recv_rim, 2, SIDES[2]),
+        copy(side_send.at[1], side_recv.at[1], send_rim, recv_rim, 3, SIDES[3]),
+    ]
+    start(border, SIDES)
     halo = [
         copy(wide.at[:, pl.ds(8, 2)], wide.at[:, pl.ds(0, 2)], send_halo, recv_halo, 0, SIDES[0]),
         copy(wide.at[:, pl.ds(2, 2)], wide.at[:, pl.ds(10, 2)], send_halo, recv_halo, 1, SIDES[1]),
@@ -171,8 +190,8 @@
     for one in loads[4:]:
         one.wait()
 
-    def exchange(turn, carry):
-        here = pl.ds(pl.multiple_of(turn * CHUNK, CHUNK), CHUNK)
+    def exchange(turn):
+        here = slice(turn * CHUNK, turn * CHUNK + CHUNK)
         cells = cell[:, here]
         goal = target[:, here]
         diameter = size[:, here]
@@ -204,13 +223,64 @@
             [hot_xy * drag_high, hot_xy * vapour_high, hot_xy * drag_low, hot_xy * vapour_low], axis=0
         ).astype(BF16)
         summed[...] += lax.dot_general(spread, hot_z, NT, preferred_element_type=F32)
-        return carry
 
     turns = slots // CHUNK
-    lax.fori_loop(0, turns // 2, exchange, 0)
+    exchange(0)
+
+    own = (pl.ds(8, 8), pl.ds(8, 8))
+    tile_row = lax.broadcasted_iota(jnp.int32, (8, 256), 0)
+
+    def layer(dx, i):
+        return 8 - i if dx > 0 else i - 1
+
+    def blocks(buffer, which, send, recv):
+        block = buffer[own]
+        for way, (dx, dy) in enumerate(CORNERS):
+            for i in range(1, 5):
+                near, far = block[layer(dx, i)], block[layer(dx, 9 - i)]
+                if i > 1:
+                    if dy > 0:
+                        near = jnp.where(tile_row >= i, near, pltpu.roll(far, i - 1, 0))
+                    else:
+                        near = jnp.where(tile_row < 8 - i, near, pltpu.roll(far, 9 - i, 0))
+                corner_send[which, way, i - 1] = near
+        copies = [
+            copy(
+                buffer.at[own], buffer.at[pl.ds(8 - 8 * dx, 8), pl.ds(8 - 8 * dy, 8)],
+                send, recv, spot, (dx, dy),
+            )
+            for spot, (dx, dy) in enumerate(SIDES)
+        ]
+        copies += [
+            copy(corner_send.at[which, way], corner_recv.at[which, way], send, recv, 4 + way, side)
+            for way, side in enumerate(CORNERS)
+        ]
+        start(copies, AROUND)
+        return copies
+
+    def unpack(buffer, which):
+        for way, (dx, dy) in enumerate(CORNERS):
+            base, side = 8 - 8 * dx, slice(8 - 8 * dy, 16 - 8 * dy)
+            for i in range(1, 5):
+                tile = corner_recv[which, way, i - 1]
+                buffer[base + layer(dx, i), side] = tile
+                back = (9 - i if dy > 0 else i - 1) % 8
+                buffer[base + layer(dx, 9 - i), side] = pltpu.roll(tile, back, 0) if back else tile
+
+    receive(border, SIDES)
+    guess[:, 7:8] = side_recv[0]
+    guess[:, 16:17] = side_recv[1]
+    sums[own] = (
+        rim[2:10] + rim[0:8] + guess[:, 9:17] + guess[:, 7:15]
+        + along_depth(rim[1:9], 1) + along_depth(rim[1:9], -1)
+    )
+    sum_copies = blocks(sums, 0, send_sum, recv_sum)
+
+    for turn in range(1, turns - 1):
+        exchange(turn)
 
     receive(halo, SIDES)
-    for f in range(6):
+    for f in range(5):
         tall[f, :, 6:8] = edge_recv[0, f]
         tall[f, :, 16:18] = edge_recv[1, f]
     for f in range(5):
@@ -238,53 +308,7 @@
             ]
             start(edges, SIDES)
 
-    own = (pl.ds(8, 8), pl.ds(8, 8))
-    tile_row = lax.broadcasted_iota(jnp.int32, (8, 256), 0)
-
-    def layer(dx, i):
-        return 8 - i if dx > 0 else i - 1
-
-    def blocks(buffer, which, send, recv):
-        block = buffer[own]
-        for way, (dx, dy) in enumerate(CORNERS):
-            for i in range(1, 5):
-                near, far = block[layer(dx, i)], block[layer(dx, 9 - i)]
-                if i > 1:
-                    if dy > 0:
-                        near = jnp.where(tile_row >= i, near, pltpu.roll(far, i - 1, 0))
-                    else:
-                        near = jnp.where(tile_row < 8 - i, near, pltpu.roll(far, 9 - i, 0))
-                corner_send[which, way, i - 1] = near
-        copies = [
-            copy(
-                buffer.at[own], buffer.at[pl.ds(8 - 8 * dx, 8), pl.ds(8 - 8 * dy, 8)],
-                send, recv, spot, (dx, dy),
-            )
-            for spot, (dx, dy) in enumerate(SIDES)
-        ]
-        copies += [
-            copy(corner_send.at[which, way], corner_recv.at[which, way], send, recv, 4 + way, side)
-            for way, side in enumerate(CORNERS)
-        ]
-        start(copies, AROUND)
-        return copies
-
-    def unpack(buffer, which):
-        for way, (dx, dy) in enumerate(CORNERS):
-            base, side = 8 - 8 * dx, slice(8 - 8 * dy, 16 - 8 * dy)
-            for i in range(1, 5):
-                tile = corner_recv[which, way, i - 1]
-                buffer[base + layer(dx, i), side] = tile
-                back = (9 - i if dy > 0 else i - 1) % 8
-                buffer[base + layer(dx, 9 - i), side] = pltpu.roll(tile, back, 0) if back else tile
-
-    sums[own] = (
-        wide[5, 3:11] + wide[5, 1:9] + tall[5, :, 9:17] + tall[5, :, 7:15]
-        + along_depth(wide[5, 2:10], 1) + along_depth(wide[5, 2:10], -1)
-    )
-    sum_copies = blocks(sums, 0, send_sum, recv_sum)
-
-    lax.fori_loop(turns // 2, turns, exchange, 0)
+    exchange(turns - 1)
 
     numbers = lax.broadcasted_iota(jnp.int32, (rows, depth), 0) * depth + lax.broadcasted_iota(
         jnp.int32, (rows, depth), 1
@@ -403,6 +427,7 @@
     late.append(pltpu.make_async_copy(arrived, arrived_hbm, send_out.at[4]))
     late[2].start()
 
+    sent(border, SIDES)
     sent(halo, SIDES)
     sent(edges, SIDES)
     sent(sum_copies, AROUND)
@@ -414,10 +439,14 @@
 
 def hand_over_kernel(*refs):
     sems = refs[-1]
-    copies = [pltpu.make_async_copy(refs[k], refs[4 + k], sems.at[k]) for k in range(4)]
-    for one in copies:
+    into = [pltpu.make_async_copy(refs[k], refs[8 + k], sems.at[k]) for k in range(4)]
+    out = [pltpu.make_async_copy(refs[8 + k], refs[4 + k], sems.at[4 + k]) for k in range(4)]
+    for one in into:
         one.start()
-    for one in copies:
+    for k in (3, 1, 2, 0):
+        into[k].wait()
+        out[k].start()
+    for one in out:
         one.wait()
 
 
@@ -457,10 +486,14 @@
             pltpu.VMEM((8, slots), F32),
             pltpu.VMEM((4, 8, 512), F32),
             pltpu.VMEM((4, 8, 512), F32),
-            pltpu.VMEM((6, 12, 8, 256), F32),
-            pltpu.VMEM((6, 8, 24, 256), F32),
-            pltpu.VMEM((2, 6, 8, 2, 256), F32),
-            pltpu.VMEM((2, 6, 8, 2, 256), F32),
+            pltpu.VMEM((8, 24, 256), F32),
+            pltpu.VMEM((10, 8, 256), F32),
+            pltpu.VMEM((2, 8, 1, 256), F32),
+            pltpu.VMEM((2, 8, 1, 256), F32),
+            pltpu.VMEM((5, 12, 8, 256), F32),
+            pltpu.VMEM((5, 8, 24, 256), F32),
+            pltpu.VMEM((2, 5, 8, 2, 256), F32),
+            pltpu.VMEM((2, 5, 8, 2, 256), F32),
             pltpu.VMEM((24, 24, 256), F32),
             pltpu.VMEM((24, 24, 256), F32),
             pltpu.VMEM((2, 4, 4, 8, 256), F32),
@@ -470,7 +503,7 @@
             pltpu.VMEM((2, 8, 1, 256), F32),
             pltpu.VMEM((2, 8, 1, 256), F32),
         ]
-        + [dma((11,)), dma((5,))] + [dma((4,))] * 6 + [dma((8,))] * 4,
+        + [dma((11,)), dma((5,))] + [dma((4,))] * 8 + [dma((8,))] * 4,
         compiler_params=pltpu.CompilerParams(
             collective_id=0, has_side_effects=True, vmem_limit_bytes=60 * 1024 * 1024
         ),
@@ -482,7 +515,7 @@
         out_shape=outs,
         in_specs=[hbm] * 4,
         out_specs=(hbm,) * 4,
-        scratch_shapes=[dma((4,))],
+        scratch_shapes=[pltpu.VMEM(one.shape, F32) for one in outs] + [dma((8,))],
         compiler_params=pltpu.CompilerParams(vmem_limit_bytes=60 * 1024 * 1024),
     )(*results)
 

time: 36.9 us -> 21.6 us (0.59)
  Pallas kernels: 36.1 us -> 20.8 us
    pallas_call x1, Pallas kernels: 16.8 us -> 1.84 us  [body(): pl.pallas_call(hand_over_kernel, out_shape=outs, in_specs=[hbm] * 4, out_...]
where the time goes in v3:
time: 21.6 us; the launch traced here: 21.5 us
  Pallas kernels  20.8 us (96%)
  between operations  0.64 us (3%)
    pallas_call x1, Pallas kernels, body(): pl.pallas_call(functools.partial(evolve_kernel, n_gx, n_gy), out_shape=ou...  19 us
    pallas_call x1, Pallas kernels, body(): pl.pallas_call(hand_over_kernel, out_shape=outs, in_specs=[hbm] * 4, out_...  1.84 us

profile of v3, /device:TPU:1, one launch (start us, length us, event | category | flops | bytes accessed | tf_op | source)
XLA Modules:
  0.0 21.5 jit_solution(4460574845848504652)
XLA Ops:
  0.6 19.0 %shard_map.120 = (f32[5,8,8,256]{3,2,1,0:T(8,128)}, f32[8,8,256]{2,1,0:T(8,128)}, f32[5,1,4096]{2,1,0:T(1,128)}, f32[4,5,1,512]{3,2,1,0:T(1,128)}) custom-call(f32[5,8,8,256]{3,2,1,0:T(8,128)} %gas_hbm.1, f32[8,8,256]{2,1,0:T(8,128)} %guess_hbm.1, f32[4,1,4096]{2,1,0:T(1,128)} %motion_hbm.1, f32[1,4096]{1,0:T(1,128)} %size_hbm.1, s32[1,4096]{1,0:T(1,128)} %cell_hbm.1, ...), custom_call_target="tpu_custom_call" | custom-call | tf_op jit(solution)/shard_map/pallas_call | solution.py:464
  19.6 1.8 %shard_map.121 = (f32[5,8,8,256]{3,2,1,0:T(8,128)}, f32[8,8,256]{2,1,0:T(8,128)}, f32[5,1,4096]{2,1,0:T(1,128)}, f32[4,5,1,512]{3,2,1,0:T(1,128)}) custom-call(f32[5,8,8,256]{3,2,1,0:T(8,128)} %get-tuple-element.8.refs_0_, f32[8,8,256]{2,1,0:T(8,128)} %get-tuple-element.9.refs_1_, f32[5,1,4096]{2,1,0:T(1,128)} %get-tuple-element.10.refs_2_, ...), custom_call_target="tpu_custom_call" | custom-call | tf_op jit(solution)/shard_map/pallas_call | solution.py:513

commit v4 on v3

--- a/solution.py
+++ b/solution.py
@@ -47,11 +47,19 @@
     return jnp.concatenate([jnp.where(inside, first, second), jnp.where(inside, second, 0.0)], axis=2)
 
 
+def along_rows(values, by):
+    row = lax.broadcasted_iota(jnp.int32, (1, 8, 256), 1)
+    edge = row == (0 if by > 0 else 7)
+    tiles = [pltpu.roll(values[:, k : k + 8], by % 8, 1) for k in range(0, values.shape[1], 8)]
+    beside = [0.0] + tiles[:-1] if by > 0 else tiles[1:] + [0.0]
+    return jnp.concatenate([jnp.where(edge, other, tile) for tile, other in zip(tiles, beside)], axis=1)
+
+
 def evolve_kernel(
     n_gx, n_gy,
     gas_hbm, guess_hbm, motion_hbm, size_hbm, cell_hbm, target_hbm, on_hbm, time_hbm, place_hbm,
     gas_next, pressure, kept_hbm, arrived_hbm,
-    star, factors, kept, arrived, swap, final,
+    star, kept, arrived, swap, final,
     motion, size, cell, target, spray_on, spray_time, spray_cell,
     grid_pieces, summed, packed, renewed, parcels, landed,
     guess, rim, side_send, side_recv, wide, tall, edge_send, edge_recv, sums, parts, corner_send, corner_recv, tall_v, u_halo, v_send, v_recv,
@@ -61,6 +69,18 @@
     me_x, me_y = lax.axis_index("gx"), lax.axis_index("gy")
     slots = size.shape[1]
     rows, depth = 64, 256
+    pair = n_gy == 2
+    tall_rows = sums.shape[1]
+    own_y = pl.multiple_of(me_y * 8, 8) if pair else 8
+    own = (pl.ds(8, 8), pl.ds(own_y, 8))
+
+    def there(dy):
+        return pl.ds(own_y, 8) if pair else pl.ds(8 - 8 * dy, 8)
+
+    def here_from(dy):
+        if pair:
+            return pl.ds(own_y if dy == 0 else pl.multiple_of((1 - me_y) * 8, 8), 8)
+        return pl.ds(8 - 8 * dy, 8)
 
     def exists(dx, dy):
         to_x, to_y = me_x + dx, me_y + dy
@@ -141,10 +161,11 @@
     for way, (dx, dy) in enumerate(SIDES):
         @pl.when(~exists(-dx, -dy))
         def _():
-            spot = (pl.ds(8 - 8 * dx, 8), pl.ds(8 - 8 * dy, 8))
             landed[way] = jnp.zeros((8, 512), F32)
-            sums[spot] = jnp.zeros((8, 8, 256), F32)
-            parts[spot] = jnp.zeros((8, 8, 256), F32)
+            if dy == 0 or not pair:
+                spot = (pl.ds(8 - 8 * dx, 8), here_from(dy))
+                sums[spot] = jnp.zeros((8, 8, 256), F32)
+                parts[spot] = jnp.zeros((8, 8, 256), F32)
 
     for way, (dx, dy) in enumerate(CORNERS):
         @pl.when(~exists(-dx, -dy))
@@ -152,12 +173,14 @@
             corner_recv[0, way] = jnp.zeros((4, 8, 256), F32)
             corner_recv[1, way] = jnp.zeros((4, 8, 256), F32)
 
-    row = lax.broadcasted_iota(jnp.int32, (24, 256), 0)
-    low_y, high_y = exists(0, -1).astype(F32), exists(0, 1).astype(F32)
-    factor = jnp.where(row < 8, low_y, jnp.where(row < 16, 1.0, high_y)) * (1.0 / 6.0)
-    factors[0] = factor * exists(-1, 0).astype(F32)
-    factors[1] = factor
-    factors[2] = factor * exists(1, 0).astype(F32)
+    low_x, high_x = exists(-1, 0).astype(F32), exists(1, 0).astype(F32)
+    if pair:
+        factors = [low_x * (1.0 / 6.0), 1.0 / 6.0, high_x * (1.0 / 6.0)]
+    else:
+        row = lax.broadcasted_iota(jnp.int32, (1, tall_rows, 256), 1)
+        low_y, high_y = exists(0, -1).astype(F32), exists(0, 1).astype(F32)
+        factor = jnp.where(row < 8, low_y, jnp.where(row < 16, 1.0, high_y)) * (1.0 / 6.0)
+        factors = [factor * low_x, factor, factor * high_x]
     summed[...] = jnp.zeros_like(summed)
     packed[...] = jnp.zeros_like(packed)
 
@@ -166,9 +189,9 @@
     side_send[0] = rim[1:9, 7:8]
     side_send[1] = rim[1:9, 0:1]
     for f in range(5):
-        own = wide[f, 2:10]
-        edge_send[0, f] = own[:, 6:8]
-        edge_send[1, f] = own[:, 0:2]
+        inner = wide[f, 2:10]
+        edge_send[0, f] = inner[:, 6:8]
+        edge_send[1, f] = inner[:, 0:2]
     pl.semaphore_wait(barrier, sum(exists(dx, dy).astype(jnp.int32) for dx, dy in AROUND))
     border = [
         copy(rim.at[8], rim.at[0], send_rim, recv_rim, 0, SIDES[0]),
@@ -227,7 +250,6 @@
     turns = slots // CHUNK
     exchange(0)
 
-    own = (pl.ds(8, 8), pl.ds(8, 8))
     tile_row = lax.broadcasted_iota(jnp.int32, (8, 256), 0)
 
     def layer(dx, i):
@@ -246,7 +268,7 @@
                 corner_send[which, way, i - 1] = near
         copies = [
             copy(
-                buffer.at[own], buffer.at[pl.ds(8 - 8 * dx, 8), pl.ds(8 - 8 * dy, 8)],
+                buffer.at[own], buffer.at[pl.ds(8 - 8 * dx, 8), there(dy)],
                 send, recv, spot, (dx, dy),
             )
             for spot, (dx, dy) in enumerate(SIDES)
@@ -260,12 +282,18 @@
 
     def unpack(buffer, which):
         for way, (dx, dy) in enumerate(CORNERS):
-            base, side = 8 - 8 * dx, slice(8 - 8 * dy, 16 - 8 * dy)
-            for i in range(1, 5):
-                tile = corner_recv[which, way, i - 1]
-                buffer[base + layer(dx, i), side] = tile
-                back = (9 - i if dy > 0 else i - 1) % 8
-                buffer[base + layer(dx, 9 - i), side] = pltpu.roll(tile, back, 0) if back else tile
+            def place():
+                base, side = 8 - 8 * dx, here_from(dy)
+                for i in range(1, 5):
+                    tile = corner_recv[which, way, i - 1]
+                    buffer[base + layer(dx, i), side] = tile
+                    back = (9 - i if dy > 0 else i - 1) % 8
+                    buffer[base + layer(dx, 9 - i), side] = pltpu.roll(tile, back, 0) if back else tile
+
+            if pair:
+                pl.when(exists(0, -dy))(place)
+            else:
+                place()
 
     receive(border, SIDES)
     guess[:, 7:8] = side_recv[0]
@@ -283,7 +311,7 @@
     for f in range(5):
         tall[f, :, 6:8] = edge_recv[0, f]
         tall[f, :, 16:18] = edge_recv[1, f]
-    for f in range(5):
+    def predict(f):
         centre = wide[f, 2:10]
         near_x, near_x2 = wide[f, 3:11], wide[f, 1:9]
         near_y, near_y2 = tall[f, :, 9:17], tall[f, :, 7:15]
@@ -294,6 +322,9 @@
         slope_z = 8.0 * (near_z - near_z2) - (along_depth(centre, -2) - along_depth(centre, 2))
         transport = (wide[0, 2:10] * slope_x + wide[1, 2:10] * slope_y + wide[2, 2:10] * slope_z) * (1.0 / 12.0)
         star[f] = centre + TIME_STEP * (DIFFUSION * laplace - transport)
+
+    for f in range(3):
+        predict(f)
         if f == 1:
             tall_v[:, 8:16] = star[1]
             v_send[0] = star[1, :, 7:8]
@@ -308,8 +339,6 @@
             ]
             start(edges, SIDES)
 
-    exchange(turns - 1)
-
     numbers = lax.broadcasted_iota(jnp.int32, (rows, depth), 0) * depth + lax.broadcasted_iota(
         jnp.int32, (rows, depth), 1
     )
@@ -318,6 +347,8 @@
     spray = jnp.zeros((rows, depth), F32)
     for head in range(spray_on.shape[1]):
         spray += jnp.where(numbers == spray_cell[:, head : head + 1], strength[:, head : head + 1], 0.0)
+    exchange(turns - 1)
+
     total = summed[...]
     drag = total[:rows] + total[2 * rows : 3 * rows]
     vapour = total[rows : 2 * rows] + total[3 * rows :]
@@ -335,6 +366,8 @@
     parts[own] = spread * (0.5 / TIME_STEP)
     part_copies = blocks(parts, 1, send_src, recv_src)
 
+    predict(3)
+    predict(4)
     star[3] = star[3] + (TIME_STEP * (-LATENT * vapour - spray)).reshape(8, 8, 256)
     star[4] = star[4] + (TIME_STEP * vapour).reshape(8, 8, 256)
 
@@ -400,21 +433,24 @@
         old, new = swap.at[(turn - 1) % 2], swap.at[turn % 2]
         x = turn
         while x < 24 - turn:
-            end = min(x + 4, 24 - turn, (x // 8 + 1) * 8)
+            end = min(x + (4 if pair else 2), 24 - turn, (x // 8 + 1) * 8)
             centre = old[x:end]
             total = old[x - 1 : end - 1] + old[x + 1 : end + 1]
-            total = total + pltpu.roll(centre, 1, 1) + pltpu.roll(centre, 23, 1)
+            total = total + along_rows(centre, 1) + along_rows(centre, -1)
             total = total + along_depth(centre, 1) + along_depth(centre, -1)
             new[x:end] = (total - parts[x:end]) * factors[x // 8]
             x = end
 
     last = swap.at[(ITERS - 1) % 2]
-    centre = last[8:16, 8:16]
+    centre = last[own]
     final[...] = centre
     half = TIME_STEP * 0.5
-    star[0] = star[0] - half * (last[9:17, 8:16] - last[7:15, 8:16])
-    star[1] = star[1] - half * (last[8:16, 9:17] - last[8:16, 7:15])
+    star[0] = star[0] - half * (last[9:17, pl.ds(own_y, 8)] - last[7:15, pl.ds(own_y, 8)])
     star[2] = star[2] - half * (along_depth(centre, -1) - along_depth(centre, 1))
+    middle = last[8:16]
+    spare = swap.at[ITERS % 2]
+    spare[8:16] = along_rows(middle, -1) - along_rows(middle, 1)
+    star[1] = star[1] - half * spare[own]
     late = [
         pltpu.make_async_copy(star.at[pl.ds(0, 3)], gas_next.at[pl.ds(0, 3)], send_out.at[2]),
         pltpu.make_async_copy(final, pressure, send_out.at[3]),
@@ -458,6 +494,7 @@
     dma = pltpu.SemaphoreType.DMA
     slots = drop_size.shape[1]
     heads = spray_on.shape[1]
+    tall_rows = 16 if n_gy == 2 else 24
     block = gas_state.shape[1:]
     shape = functools.partial(jax.ShapeDtypeStruct, dtype=F32)
     outs = (shape(gas_state.shape), shape(block), shape((5, 1, slots)), shape((4, 5, 1, 512)))
@@ -468,10 +505,9 @@
         out_specs=(hbm,) * 4,
         scratch_shapes=[
             pltpu.VMEM(gas_state.shape, F32),
-            pltpu.VMEM((3, 24, 256), F32),
             pltpu.VMEM((5, 1, slots), F32),
             pltpu.VMEM((4, 5, 1, 512), F32),
-            pltpu.VMEM((2, 24, 24, 256), F32),
+            pltpu.VMEM((2, 24, tall_rows, 256), F32),
             pltpu.VMEM(block, F32),
             pltpu.VMEM(drop_motion.shape, F32),
             pltpu.VMEM((1, slots), F32),
@@ -494,8 +530,8 @@
             pltpu.VMEM((5, 8, 24, 256), F32),
             pltpu.VMEM((2, 5, 8, 2, 256), F32),
             pltpu.VMEM((2, 5, 8, 2, 256), F32),
-            pltpu.VMEM((24, 24, 256), F32),
-            pltpu.VMEM((24, 24, 256), F32),
+            pltpu.VMEM((24, tall_rows, 256), F32),
+            pltpu.VMEM((24, tall_rows, 256), F32),
             pltpu.VMEM((2, 4, 4, 8, 256), F32),
             pltpu.VMEM((2, 4, 4, 8, 256), F32),
             pltpu.VMEM((8, 24, 256), F32),

time: 21.6 us -> 21.2 us (0.981)
  Pallas kernels: 20.8 us -> 20.4 us
    pallas_call x1, Pallas kernels: 19 us -> 18.5 us  [body(): pl.pallas_call(functools.partial(evolve_kernel, n_gx, n_gy), out_shape=ou...]
where the time goes in v4:
time: 21.2 us; the launch traced here: 21 us
  Pallas kernels  20.4 us (96%)
  between operations  0.64 us (3%)
    pallas_call x1, Pallas kernels, body(): pl.pallas_call(functools.partial(evolve_kernel, n_gx, n_gy), out_shape=ou...  18.5 us
    pallas_call x1, Pallas kernels, body(): pl.pallas_call(hand_over_kernel, out_shape=outs, in_specs=[hbm] * 4, out_...  1.84 us

profile of v4, /device:TPU:1, one launch (start us, length us, event | category | flops | bytes accessed | tf_op | source)
XLA Modules:
  0.0 21.0 jit_solution(3688759220371476503)
XLA Ops:
  0.6 18.5 %shard_map.120 = (f32[5,8,8,256]{3,2,1,0:T(8,128)}, f32[8,8,256]{2,1,0:T(8,128)}, f32[5,1,4096]{2,1,0:T(1,128)}, f32[4,5,1,512]{3,2,1,0:T(1,128)}) custom-call(f32[5,8,8,256]{3,2,1,0:T(8,128)} %gas_hbm.1, f32[8,8,256]{2,1,0:T(8,128)} %guess_hbm.1, f32[4,1,4096]{2,1,0:T(1,128)} %motion_hbm.1, f32[1,4096]{1,0:T(1,128)} %size_hbm.1, s32[1,4096]{1,0:T(1,128)} %cell_hbm.1, ...), custom_call_target="tpu_custom_call" | custom-call | tf_op jit(solution)/shard_map/pallas_call | solution.py:501
  19.2 1.8 %shard_map.121 = (f32[5,8,8,256]{3,2,1,0:T(8,128)}, f32[8,8,256]{2,1,0:T(8,128)}, f32[5,1,4096]{2,1,0:T(1,128)}, f32[4,5,1,512]{3,2,1,0:T(1,128)}) custom-call(f32[5,8,8,256]{3,2,1,0:T(8,128)} %get-tuple-element.8.refs_0_, f32[8,8,256]{2,1,0:T(8,128)} %get-tuple-element.9.refs_1_, f32[5,1,4096]{2,1,0:T(1,128)} %get-tuple-element.10.refs_2_, ...), custom_call_target="tpu_custom_call" | custom-call | tf_op jit(solution)/shard_map/pallas_call | solution.py:549

commit v5 on v4

--- a/solution.py
+++ b/solution.py
@@ -223,8 +223,9 @@
         at_xy = lax.shift_right_logical(cells, 8)
         hot_z = (lax.broadcasted_iota(jnp.int32, (depth, CHUNK), 0) == at_z).astype(F32).astype(BF16)
         hot_xy = (lax.broadcasted_iota(jnp.int32, (rows, CHUNK), 0) == at_xy).astype(F32)
-        found = jnp.dot(grid_pieces[...], hot_z, preferred_element_type=F32)
-        found = found[: 4 * rows] + found[4 * rows :]
+        found = jnp.dot(grid_pieces[0:256], hot_z, preferred_element_type=F32) + jnp.dot(
+            grid_pieces[256:512], hot_z, preferred_element_type=F32
+        )
         local = jnp.concatenate(
             [jnp.sum(found[f * rows : (f + 1) * rows] * hot_xy, axis=0, keepdims=True) for f in range(4)], axis=0
         )
@@ -256,6 +257,11 @@
         return 8 - i if dx > 0 else i - 1
 
     def blocks(buffer, which, send, recv):
+        copies = [
+            copy(buffer.at[own], buffer.at[pl.ds(8 - 8 * dx, 8), there(dy)], send, recv, spot, (dx, dy))
+            for spot, (dx, dy) in enumerate(SIDES)
+        ]
+        start(copies[2:] + copies[:2], SIDES[2:] + SIDES[:2])
         block = buffer[own]
         for way, (dx, dy) in enumerate(CORNERS):
             for i in range(1, 5):
@@ -266,19 +272,12 @@
                     else:
                         near = jnp.where(tile_row < 8 - i, near, pltpu.roll(far, 9 - i, 0))
                 corner_send[which, way, i - 1] = near
-        copies = [
-            copy(
-                buffer.at[own], buffer.at[pl.ds(8 - 8 * dx, 8), there(dy)],
-                send, recv, spot, (dx, dy),
-            )
-            for spot, (dx, dy) in enumerate(SIDES)
-        ]
-        copies += [
+        corners = [
             copy(corner_send.at[which, way], corner_recv.at[which, way], send, recv, 4 + way, side)
             for way, side in enumerate(CORNERS)
         ]
-        start(copies, AROUND)
-        return copies
+        start(corners, CORNERS)
+        return copies + corners
 
     def unpack(buffer, which):
         for way, (dx, dy) in enumerate(CORNERS):
@@ -384,7 +383,7 @@
     eight = lax.broadcasted_iota(jnp.int32, (8, 256), 0)
 
     def pack(turn, carry):
-        here = pl.ds(pl.multiple_of(turn * CHUNK, CHUNK), CHUNK)
+        here = slice(turn * CHUNK, turn * CHUNK + CHUNK)
         goal = target[:, here]
         pieces = [(eight == goal[:, k * 256 : k * 256 + 256]).astype(F32) for k in range(CHUNK // 256)]
         counts = jnp.dot(jnp.concatenate(pieces, axis=0).astype(BF16), upper, preferred_element_type=F32)
@@ -408,7 +407,9 @@
         packed[...] += lax.dot_general(bundle, hot_low, NT, preferred_element_type=F32)
         return carry
 
-    lax.fori_loop(0, turns, pack, jnp.zeros((8, 1), F32))
+    carry = jnp.zeros((8, 1), F32)
+    for turn in range(turns):
+        carry = pack(turn, carry)
     bundle = packed[0:40] + packed[40:80]
     for f in range(5):
         for way in range(4):

time: 21.2 us -> 21.3 us (level)
  no operation moved by 1% of the time
where the time goes in v5:
time: 21.3 us; the launch traced here: 21.1 us
  Pallas kernels  20.5 us (96%)
  between operations  0.64 us (3%)
    pallas_call x1, Pallas kernels, body(): pl.pallas_call(functools.partial(evolve_kernel, n_gx, n_gy), out_shape=ou...  18.7 us
    pallas_call x1, Pallas kernels, body(): pl.pallas_call(hand_over_kernel, out_shape=outs, in_specs=[hbm] * 4, out_...  1.84 us

profile of v5, /device:TPU:1, one launch (start us, length us, event | category | flops | bytes accessed | tf_op | source)
XLA Modules:
  0.0 21.1 jit_solution(6647343366027412372)
XLA Ops:
  0.6 18.7 %shard_map.120 = (f32[5,8,8,256]{3,2,1,0:T(8,128)}, f32[8,8,256]{2,1,0:T(8,128)}, f32[5,1,4096]{2,1,0:T(1,128)}, f32[4,5,1,512]{3,2,1,0:T(1,128)}) custom-call(f32[5,8,8,256]{3,2,1,0:T(8,128)} %gas_hbm.1, f32[8,8,256]{2,1,0:T(8,128)} %guess_hbm.1, f32[4,1,4096]{2,1,0:T(1,128)} %motion_hbm.1, f32[1,4096]{1,0:T(1,128)} %size_hbm.1, s32[1,4096]{1,0:T(1,128)} %cell_hbm.1, ...), custom_call_target="tpu_custom_call" | custom-call | tf_op jit(solution)/shard_map/pallas_call | solution.py:502
  19.3 1.8 %shard_map.121 = (f32[5,8,8,256]{3,2,1,0:T(8,128)}, f32[8,8,256]{2,1,0:T(8,128)}, f32[5,1,4096]{2,1,0:T(1,128)}, f32[4,5,1,512]{3,2,1,0:T(1,128)}) custom-call(f32[5,8,8,256]{3,2,1,0:T(8,128)} %get-tuple-element.8.refs_0_, f32[8,8,256]{2,1,0:T(8,128)} %get-tuple-element.9.refs_1_, f32[5,1,4096]{2,1,0:T(1,128)} %get-tuple-element.10.refs_2_, ...), custom_call_target="tpu_custom_call" | custom-call | tf_op jit(solution)/shard_map/pallas_call | solution.py:550

commit v6 on v5

--- a/solution.py
+++ b/solution.py
@@ -303,7 +303,7 @@
     )
     sum_copies = blocks(sums, 0, send_sum, recv_sum)
 
-    for turn in range(1, turns - 1):
+    for turn in range(1, turns // 2):
         exchange(turn)
 
     receive(halo, SIDES)
@@ -346,7 +346,8 @@
     spray = jnp.zeros((rows, depth), F32)
     for head in range(spray_on.shape[1]):
         spray += jnp.where(numbers == spray_cell[:, head : head + 1], strength[:, head : head + 1], 0.0)
-    exchange(turns - 1)
+    for turn in range(max(1, turns // 2), turns):
+        exchange(turn)
 
     total = summed[...]
     drag = total[:rows] + total[2 * rows : 3 * rows]

time: 21.3 us -> 21.3 us (level)
  no operation moved by 1% of the time
where the time goes in v6:
time: 21.3 us; the launch traced here: 21.1 us
  Pallas kernels  20.5 us (96%)
  between operations  0.64 us (3%)
    pallas_call x1, Pallas kernels, body(): pl.pallas_call(functools.partial(evolve_kernel, n_gx, n_gy), out_shape=ou...  18.7 us
    pallas_call x1, Pallas kernels, body(): pl.pallas_call(hand_over_kernel, out_shape=outs, in_specs=[hbm] * 4, out_...  1.84 us

profile of v6, /device:TPU:1, one launch (start us, length us, event | category | flops | bytes accessed | tf_op | source)
XLA Modules:
  0.0 21.1 jit_solution(5275267334576140086)
XLA Ops:
  0.6 18.7 %shard_map.120 = (f32[5,8,8,256]{3,2,1,0:T(8,128)}, f32[8,8,256]{2,1,0:T(8,128)}, f32[5,1,4096]{2,1,0:T(1,128)}, f32[4,5,1,512]{3,2,1,0:T(1,128)}) custom-call(f32[5,8,8,256]{3,2,1,0:T(8,128)} %gas_hbm.1, f32[8,8,256]{2,1,0:T(8,128)} %guess_hbm.1, f32[4,1,4096]{2,1,0:T(1,128)} %motion_hbm.1, f32[1,4096]{1,0:T(1,128)} %size_hbm.1, s32[1,4096]{1,0:T(1,128)} %cell_hbm.1, ...), custom_call_target="tpu_custom_call" | custom-call | tf_op jit(solution)/shard_map/pallas_call | solution.py:503
  19.3 1.8 %shard_map.121 = (f32[5,8,8,256]{3,2,1,0:T(8,128)}, f32[8,8,256]{2,1,0:T(8,128)}, f32[5,1,4096]{2,1,0:T(1,128)}, f32[4,5,1,512]{3,2,1,0:T(1,128)}) custom-call(f32[5,8,8,256]{3,2,1,0:T(8,128)} %get-tuple-element.8.refs_0_, f32[8,8,256]{2,1,0:T(8,128)} %get-tuple-element.9.refs_1_, f32[5,1,4096]{2,1,0:T(1,128)} %get-tuple-element.10.refs_2_, ...), custom_call_target="tpu_custom_call" | custom-call | tf_op jit(solution)/shard_map/pallas_call | solution.py:551
